TPU v7x, 32 devices: a whole 2x2x4 slice. The times are simulated.
32 devices in a mesh: dp: 8 (over z, x), fsdp: 4 (over y, core).
Axes of the slice: x: 2, y: 2, z: 4, core: 2. Of those that a mesh axis runs over, the one named last changes fastest.
Arguments:
- char_inputs: bfloat16 [16, 1024, 16, 256], P('dp', 'fsdp'), may hold values from -6 to 6
- language_ids: int32 [16], P('dp'), may hold values from 0 to 31
- char_counts: int32 [16, 1024], P('dp', 'fsdp'), may hold values from 1 to 16
- row_lengths: int32 [16], P('dp'), may hold values from 512 to 1024, as said below
- cotangent: bfloat16 [16, 1024, 512], P('dp', 'fsdp'), may hold values from -6 to 6
- language_table: bfloat16 [32, 256], P(None, ('dp', 'fsdp')), may hold values from -3 to 3
- char_gain_one: bfloat16 [256], P(('dp', 'fsdp')), may hold values from 0.5 to 1.5
- char_bias_one: bfloat16 [256], P(('dp', 'fsdp')), may hold values from -1 to 1
- char_inward: bfloat16 [256, 768], P(('dp', 'fsdp')), may hold values from -0.375 to 0.375
- char_outward: bfloat16 [256, 256], P(('dp', 'fsdp')), may hold values from -0.75 to 0.75
- char_gain_two: bfloat16 [256], P(('dp', 'fsdp')), may hold values from 0.5 to 1.5
- char_bias_two: bfloat16 [256], P(('dp', 'fsdp')), may hold values from -1 to 1
- char_expand: bfloat16 [256, 1024], P(('dp', 'fsdp')), may hold values from -0.375 to 0.375
- char_expand_bias: bfloat16 [1024], P(('dp', 'fsdp')), may hold values from -1 to 1
- char_reduce: bfloat16 [1024, 256], P(('dp', 'fsdp')), may hold values from -0.1875 to 0.1875
- char_reduce_bias: bfloat16 [256], P(('dp', 'fsdp')), may hold values from -1 to 1
- char_to_word: bfloat16 [256, 512], P(('dp', 'fsdp')), may hold values from -0.375 to 0.375
- char_to_word_bias: bfloat16 [512], P(('dp', 'fsdp')), may hold values from -1 to 1
- word_gain_one: bfloat16 [512], P(('dp', 'fsdp')), may hold values from 0.5 to 1.5
- word_bias_one: bfloat16 [512], P(('dp', 'fsdp')), may hold values from -1 to 1
- word_inward: bfloat16 [512, 1536], P(('dp', 'fsdp')), may hold values from -0.25 to 0.25
- word_outward: bfloat16 [512, 512], P(('dp', 'fsdp')), may hold values from -1 to 1
- word_gain_two: bfloat16 [512], P(('dp', 'fsdp')), may hold values from 0.5 to 1.5
- word_bias_two: bfloat16 [512], P(('dp', 'fsdp')), may hold values from -1 to 1
- word_expand: bfloat16 [512, 2048], P(('dp', 'fsdp')), may hold values from -0.25 to 0.25
- word_expand_bias: bfloat16 [2048], P(('dp', 'fsdp')), may hold values from -1 to 1
- word_reduce: bfloat16 [2048, 512], P(('dp', 'fsdp')), may hold values from -0.125 to 0.125
- word_reduce_bias: bfloat16 [512], P(('dp', 'fsdp')), may hold values from -1 to 1
Outputs:
- words_out: float32 [16, 1024, 512], P('dp', 'fsdp')
- char_input_grad: float32 [16, 1024, 16, 256], P('dp', 'fsdp')
- grad_language_table: float32 [32, 256], P(None, ('dp', 'fsdp'))
- grad_char_gain_one: float32 [256], P(('dp', 'fsdp'))
- grad_char_bias_one: float32 [256], P(('dp', 'fsdp'))
- grad_char_inward: float32 [256, 768], P(('dp', 'fsdp'))
- grad_char_outward: float32 [256, 256], P(('dp', 'fsdp'))
- grad_char_gain_two: float32 [256], P(('dp', 'fsdp'))
- grad_char_bias_two: float32 [256], P(('dp', 'fsdp'))
- grad_char_expand: float32 [256, 1024], P(('dp', 'fsdp'))
- grad_char_expand_bias: float32 [1024], P(('dp', 'fsdp'))
- grad_char_reduce: float32 [1024, 256], P(('dp', 'fsdp'))
- grad_char_reduce_bias: float32 [256], P(('dp', 'fsdp'))
- grad_char_to_word: float32 [256, 512], P(('dp', 'fsdp'))
- grad_char_to_word_bias: float32 [512], P(('dp', 'fsdp'))
- grad_word_gain_one: float32 [512], P(('dp', 'fsdp'))
- grad_word_bias_one: float32 [512], P(('dp', 'fsdp'))
- grad_word_inward: float32 [512, 1536], P(('dp', 'fsdp'))
- grad_word_outward: float32 [512, 512], P(('dp', 'fsdp'))
- grad_word_gain_two: float32 [512], P(('dp', 'fsdp'))
- grad_word_bias_two: float32 [512], P(('dp', 'fsdp'))
- grad_word_expand: float32 [512, 2048], P(('dp', 'fsdp'))
- grad_word_expand_bias: float32 [2048], P(('dp', 'fsdp'))
- grad_word_reduce: float32 [2048, 512], P(('dp', 'fsdp'))
- grad_word_reduce_bias: float32 [512], P(('dp', 'fsdp'))
Inputs may be any that keep to these rules, and one draw needn't show every extreme that they name: `row_lengths`: in each aligned group of 2 rows one row has all 1024 words. The live characters of a word are its first char_counts ones.
All inputs are finite; a program needn't handle non-finite values.
Results may differ from a plain program's by a relative error of at most 0.013.
Values may be sent and summed in bfloat16 or wider, within the bound.
No kernel may reach another device: no remote copies, remote signals or barrier semaphores. Data moves between devices by JAX's collectives and lax.ppermute only.
A program may use at most 384 MiB of HBM per device.

v0:
```python
import jax
import jax.numpy as jnp
from jax import lax
from jax.sharding import PartitionSpec as P

CHEADS = 4
WHEADS = 8


EPS = 1e-05
NEG_BIG = -1000000000.0
HIGHEST = lax.Precision.HIGHEST


def product(left_side, right_side):
    return jnp.dot(left_side, right_side, preferred_element_type=jnp.float32)


def back_product(grad_low, weight):
    return lax.dot_general(
        grad_low,
        weight,
        (((grad_low.ndim - 1,), (1,)), ((), ())),
        preferred_element_type=jnp.float32,
    )


def weight_grad(left_side, right_side):
    flat_left = left_side.reshape(-1, left_side.shape[-1])
    flat_right = right_side.reshape(-1, right_side.shape[-1])
    return lax.dot_general(
        flat_left, flat_right, (((0,), (0,)), ((), ())), preferred_element_type=jnp.float32
    )


def norm_apply(hidden, norm_gain, norm_bias):
    row_mean = jnp.mean(hidden, -1, keepdims=True)
    centred = hidden - row_mean
    variance = jnp.mean(centred * centred, -1, keepdims=True)
    return centred * lax.rsqrt(variance + EPS) * norm_gain + norm_bias


def norm_back(hidden, norm_gain, norm_bias, upstream):
    outputs, pullback = jax.vjp(norm_apply, hidden, norm_gain, norm_bias)
    return pullback(upstream)


def gelu_back(pre_gelu, upstream):
    outputs, pullback = jax.vjp(jax.nn.gelu, pre_gelu)
    return pullback(upstream)[0]


def char_pass(weights, char_inputs, language_ids, char_counts):
    (
        table,
        gain_one,
        bias_one,
        inward,
        outward,
        gain_two,
        bias_two,
        expand,
        expand_bias,
        reduce_weight,
        reduce_bias,
        to_word,
        to_word_bias,
    ) = weights
    row_count, local_words, char_len, features = char_inputs.shape
    word_count = row_count * local_words
    head_size = features // CHEADS
    score_scale = head_size ** (-0.5)
    one_hot = (language_ids[:, None] == jnp.arange(table.shape[0])[None, :]).astype(jnp.bfloat16)
    language_rows = product(one_hot, table)
    char_start = (char_inputs.astype(jnp.float32) + language_rows[:, None, None, :]).reshape(
        word_count, char_len, features
    )
    live_mask = jnp.arange(char_len)[None, :] < char_counts.reshape(word_count)[:, None]
    normed = norm_apply(
        char_start, gain_one.astype(jnp.float32), bias_one.astype(jnp.float32)
    ).astype(jnp.bfloat16)
    projected = product(normed, inward).astype(jnp.bfloat16)
    queries = projected[..., :features].reshape(word_count, char_len, CHEADS, head_size)
    key_rows = projected[..., features : 2 * features].reshape(
        word_count, char_len, CHEADS, head_size
    )
    values = projected[..., 2 * features :].reshape(word_count, char_len, CHEADS, head_size)
    scores = (
        jnp.einsum("nchx,ndhx->hcdn", queries, key_rows, preferred_element_type=jnp.float32)
        * score_scale
    )
    scores = jnp.where(live_mask.T[None, None], scores, NEG_BIG)
    soft_weights = jax.nn.softmax(scores, axis=2)
    soft_low = soft_weights.astype(jnp.bfloat16)
    mixed_low = jnp.einsum("hcdn,ndhx->nchx", soft_low, values, preferred_element_type=jnp.float32)
    mixed_low = mixed_low.reshape(word_count, char_len, features).astype(jnp.bfloat16)
    after_attn = char_start + product(mixed_low, outward)
    normed_two = norm_apply(
        after_attn, gain_two.astype(jnp.float32), bias_two.astype(jnp.float32)
    ).astype(jnp.bfloat16)
    pre_gelu = product(normed_two, expand) + expand_bias.astype(jnp.float32)
    activated = jax.nn.gelu(pre_gelu).astype(jnp.bfloat16)
    after_mlp = after_attn + (product(activated, reduce_weight) + reduce_bias.astype(jnp.float32))
    live_float = live_mask.astype(jnp.float32)
    counts_float = char_counts.reshape(word_count).astype(jnp.float32)
    pooled = (jnp.sum(after_mlp * live_float[..., None], 1) / counts_float[:, None]).astype(
        jnp.bfloat16
    )
    word_in = product(pooled, to_word) + to_word_bias.astype(jnp.float32)
    return (
        one_hot,
        char_start,
        live_float,
        counts_float,
        normed,
        queries,
        key_rows,
        values,
        soft_weights,
        soft_low,
        mixed_low,
        after_attn,
        normed_two,
        pre_gelu,
        activated,
        pooled,
        word_in,
    )


def char_back(weights, saved_state, grad_word_in, char_shape):
    (
        table,
        gain_one,
        bias_one,
        inward,
        outward,
        gain_two,
        bias_two,
        expand,
        expand_bias,
        reduce_weight,
        reduce_bias,
        to_word,
        to_word_bias,
    ) = weights
    (
        one_hot,
        char_start,
        live_float,
        counts_float,
        normed,
        queries,
        key_rows,
        values,
        soft_weights,
        soft_low,
        mixed_low,
        after_attn,
        normed_two,
        pre_gelu,
        activated,
        pooled,
        word_in,
    ) = saved_state
    row_count, local_words, char_len, features = char_shape
    word_count = row_count * local_words
    head_size = features // CHEADS
    score_scale = head_size ** (-0.5)
    word_in_low = grad_word_in.astype(jnp.bfloat16)
    grad_to_word = weight_grad(pooled, word_in_low)
    grad_to_word_bias = jnp.sum(word_in_low.astype(jnp.float32), 0)
    grad_pooled = back_product(word_in_low, to_word)
    grad_out = (grad_pooled / counts_float[:, None])[:, None, :] * live_float[..., None]
    grad_out_low = grad_out.astype(jnp.bfloat16)
    grad_reduce = weight_grad(activated, grad_out_low)
    grad_reduce_bias = jnp.sum(grad_out_low.astype(jnp.float32), (0, 1))
    grad_pre = gelu_back(pre_gelu, back_product(grad_out_low, reduce_weight)).astype(jnp.bfloat16)
    grad_expand = weight_grad(normed_two, grad_pre)
    grad_expand_bias = jnp.sum(grad_pre.astype(jnp.float32), (0, 1))
    grad_attn, grad_gain_two, grad_bias_two = norm_back(
        after_attn,
        gain_two.astype(jnp.float32),
        bias_two.astype(jnp.float32),
        back_product(grad_pre, expand),
    )
    grad_attn = grad_out + grad_attn
    grad_attn_low = grad_attn.astype(jnp.bfloat16)
    grad_outward = weight_grad(mixed_low, grad_attn_low)
    grad_mixed = (
        back_product(grad_attn_low, outward)
        .astype(jnp.bfloat16)
        .reshape(word_count, char_len, CHEADS, head_size)
    )
    grad_soft = jnp.einsum(
        "nchx,ndhx->hcdn", grad_mixed, values, preferred_element_type=jnp.float32
    )
    grad_scores = (
        soft_weights * (grad_soft - jnp.sum(soft_weights * grad_soft, 2, keepdims=True))
    ).astype(jnp.bfloat16)
    grad_queries = (
        jnp.einsum("hcdn,ndhx->nchx", grad_scores, key_rows, preferred_element_type=jnp.float32)
        * score_scale
    )
    grad_keys = (
        jnp.einsum("hcdn,nchx->ndhx", grad_scores, queries, preferred_element_type=jnp.float32)
        * score_scale
    )
    grad_values = jnp.einsum(
        "hcdn,nchx->ndhx", soft_low, grad_mixed, preferred_element_type=jnp.float32
    )
    grad_projected = jnp.concatenate(
        [
            grad_queries.reshape(word_count, char_len, features),
            grad_keys.reshape(word_count, char_len, features),
            grad_values.reshape(word_count, char_len, features),
        ],
        -1,
    ).astype(jnp.bfloat16)
    grad_inward = weight_grad(normed, grad_projected)
    grad_start, grad_gain_one, grad_bias_one = norm_back(
        char_start,
        gain_one.astype(jnp.float32),
        bias_one.astype(jnp.float32),
        back_product(grad_projected, inward),
    )
    grad_start = grad_attn + grad_start
    per_row = jnp.sum(grad_start.reshape(row_count, local_words * char_len, features), 1)
    grad_table = lax.dot_general(
        one_hot.astype(jnp.float32), per_row, (((0,), (0,)), ((), ())), precision=HIGHEST
    )
    grads = (
        grad_table,
        grad_gain_one,
        grad_bias_one,
        grad_inward,
        grad_outward,
        grad_gain_two,
        grad_bias_two,
        grad_expand,
        grad_expand_bias,
        grad_reduce,
        grad_reduce_bias,
        grad_to_word,
        grad_to_word_bias,
    )
    return (grad_start.reshape(row_count, local_words, char_len, features), grads)


def word_scores(queries, key_gathered, allowed, score_scale):
    scores = (
        jnp.einsum("rihx,rjhx->rhij", queries, key_gathered, preferred_element_type=jnp.float32)
        * score_scale
    )
    return jnp.where(allowed[:, None], scores, NEG_BIG)


def word_pass(weights, word_in, row_lengths):
    (
        gain_one,
        bias_one,
        inward,
        outward,
        gain_two,
        bias_two,
        expand,
        expand_bias,
        reduce_weight,
        reduce_bias,
    ) = weights
    row_count, local_words, features = word_in.shape
    head_size = features // WHEADS
    score_scale = head_size ** (-0.5)
    normed = norm_apply(word_in, gain_one.astype(jnp.float32), bias_one.astype(jnp.float32)).astype(
        jnp.bfloat16
    )
    projected = product(normed, inward).astype(jnp.bfloat16)
    queries = projected[..., :features].reshape(row_count, local_words, WHEADS, head_size)
    pair_gathered = lax.all_gather(projected[..., features:], "fsdp", axis=1, tiled=True)
    total_words = pair_gathered.shape[1]
    key_gathered = pair_gathered[..., :features].reshape(row_count, total_words, WHEADS, head_size)
    value_gathered = pair_gathered[..., features:].reshape(
        row_count, total_words, WHEADS, head_size
    )
    query_index = lax.axis_index("fsdp") * local_words + jnp.arange(local_words)
    key_index = jnp.arange(total_words)
    allowed = (key_index[None, None, :] <= query_index[None, :, None]) & (
        key_index[None, None, :] < row_lengths[:, None, None]
    )
    scores = word_scores(queries, key_gathered, allowed, score_scale)
    row_max = jnp.max(scores, -1, keepdims=True)
    exponent = jnp.exp(scores - row_max)
    row_total = jnp.sum(exponent, -1, keepdims=True)
    soft_low = (exponent / row_total).astype(jnp.bfloat16)
    log_total = row_max + jnp.log(row_total)
    mixed_low = jnp.einsum(
        "rhij,rjhx->rihx", soft_low, value_gathered, preferred_element_type=jnp.float32
    )
    mixed_low = mixed_low.reshape(row_count, local_words, features).astype(jnp.bfloat16)
    after_attn = word_in + product(mixed_low, outward)
    normed_two = norm_apply(
        after_attn, gain_two.astype(jnp.float32), bias_two.astype(jnp.float32)
    ).astype(jnp.bfloat16)
    pre_gelu = product(normed_two, expand) + expand_bias.astype(jnp.float32)
    activated = jax.nn.gelu(pre_gelu).astype(jnp.bfloat16)
    after_mlp = after_attn + (product(activated, reduce_weight) + reduce_bias.astype(jnp.float32))
    valid_mask = query_index[None, :] < row_lengths[:, None]
    words_out = jnp.where(valid_mask[..., None], after_mlp, 0.0)
    saved_state = (
        normed,
        queries,
        key_gathered,
        value_gathered,
        allowed,
        log_total,
        mixed_low,
        after_attn,
        normed_two,
        pre_gelu,
        activated,
        valid_mask,
    )
    return (saved_state, words_out)


def word_back(weights, word_in, saved_state, cotangent):
    (
        gain_one,
        bias_one,
        inward,
        outward,
        gain_two,
        bias_two,
        expand,
        expand_bias,
        reduce_weight,
        reduce_bias,
    ) = weights
    (
        normed,
        queries,
        key_gathered,
        value_gathered,
        allowed,
        log_total,
        mixed_low,
        after_attn,
        normed_two,
        pre_gelu,
        activated,
        valid_mask,
    ) = saved_state
    row_count, local_words, features = word_in.shape
    total_words = key_gathered.shape[1]
    head_size = features // WHEADS
    score_scale = head_size ** (-0.5)
    upstream = jnp.where(valid_mask[..., None], cotangent.astype(jnp.float32), 0.0)
    upstream_low = upstream.astype(jnp.bfloat16)
    grad_reduce = weight_grad(activated, upstream_low)
    grad_reduce_bias = jnp.sum(upstream_low.astype(jnp.float32), (0, 1))
    grad_pre = gelu_back(pre_gelu, back_product(upstream_low, reduce_weight)).astype(jnp.bfloat16)
    grad_expand = weight_grad(normed_two, grad_pre)
    grad_expand_bias = jnp.sum(grad_pre.astype(jnp.float32), (0, 1))
    grad_attn, grad_gain_two, grad_bias_two = norm_back(
        after_attn,
        gain_two.astype(jnp.float32),
        bias_two.astype(jnp.float32),
        back_product(grad_pre, expand),
    )
    grad_attn = upstream + grad_attn
    grad_attn_low = grad_attn.astype(jnp.bfloat16)
    grad_outward = weight_grad(mixed_low, grad_attn_low)
    grad_mixed = (
        back_product(grad_attn_low, outward)
        .astype(jnp.bfloat16)
        .reshape(row_count, local_words, WHEADS, head_size)
    )
    scores = word_scores(queries, key_gathered, allowed, score_scale)
    soft_weights = jnp.exp(scores - log_total)
    grad_soft = jnp.einsum(
        "rihx,rjhx->rhij", grad_mixed, value_gathered, preferred_element_type=jnp.float32
    )
    soft_dot = jnp.sum(soft_weights * grad_soft, -1, keepdims=True)
    grad_scores = (soft_weights * (grad_soft - soft_dot)).astype(jnp.bfloat16)
    grad_queries = (
        jnp.einsum("rhij,rjhx->rihx", grad_scores, key_gathered, preferred_element_type=jnp.float32)
        * score_scale
    )
    soft_low = soft_weights.astype(jnp.bfloat16)
    grad_keys = (
        jnp.einsum("rhij,rihx->rjhx", grad_scores, queries, preferred_element_type=jnp.float32)
        * score_scale
    )
    grad_values = jnp.einsum(
        "rhij,rihx->rjhx", soft_low, grad_mixed, preferred_element_type=jnp.float32
    )
    grad_pair = jnp.concatenate(
        [
            grad_keys.reshape(row_count, total_words, features),
            grad_values.reshape(row_count, total_words, features),
        ],
        -1,
    )
    grad_pair_own = lax.psum_scatter(
        grad_pair.astype(jnp.bfloat16), "fsdp", scatter_dimension=1, tiled=True
    ).astype(jnp.float32)
    grad_projected = jnp.concatenate(
        [grad_queries.reshape(row_count, local_words, features), grad_pair_own], -1
    ).astype(jnp.bfloat16)
    grad_inward = weight_grad(normed, grad_projected)
    grad_input, grad_gain_one, grad_bias_one = norm_back(
        word_in,
        gain_one.astype(jnp.float32),
        bias_one.astype(jnp.float32),
        back_product(grad_projected, inward),
    )
    grads = (
        grad_gain_one,
        grad_bias_one,
        grad_inward,
        grad_outward,
        grad_gain_two,
        grad_bias_two,
        grad_expand,
        grad_expand_bias,
        grad_reduce,
        grad_reduce_bias,
    )
    return (grad_attn + grad_input, grads)


def body(
    char_inputs,
    language_ids,
    char_counts,
    row_lengths,
    cotangent,
    language_table,
    char_gain_one,
    char_bias_one,
    char_inward,
    char_outward,
    char_gain_two,
    char_bias_two,
    char_expand,
    char_expand_bias,
    char_reduce,
    char_reduce_bias,
    char_to_word,
    char_to_word_bias,
    word_gain_one,
    word_bias_one,
    word_inward,
    word_outward,
    word_gain_two,
    word_bias_two,
    word_expand,
    word_expand_bias,
    word_reduce,
    word_reduce_bias,
):
    char_full = (
        lax.all_gather(language_table, ("dp", "fsdp"), axis=1, tiled=True),
        lax.all_gather(char_gain_one, ("dp", "fsdp"), axis=0, tiled=True),
        lax.all_gather(char_bias_one, ("dp", "fsdp"), axis=0, tiled=True),
        lax.all_gather(char_inward, ("dp", "fsdp"), axis=0, tiled=True),
        lax.all_gather(char_outward, ("dp", "fsdp"), axis=0, tiled=True),
        lax.all_gather(char_gain_two, ("dp", "fsdp"), axis=0, tiled=True),
        lax.all_gather(char_bias_two, ("dp", "fsdp"), axis=0, tiled=True),
        lax.all_gather(char_expand, ("dp", "fsdp"), axis=0, tiled=True),
        lax.all_gather(char_expand_bias, ("dp", "fsdp"), axis=0, tiled=True),
        lax.all_gather(char_reduce, ("dp", "fsdp"), axis=0, tiled=True),
        lax.all_gather(char_reduce_bias, ("dp", "fsdp"), axis=0, tiled=True),
        lax.all_gather(char_to_word, ("dp", "fsdp"), axis=0, tiled=True),
        lax.all_gather(char_to_word_bias, ("dp", "fsdp"), axis=0, tiled=True),
    )
    word_full = (
        lax.all_gather(word_gain_one, ("dp", "fsdp"), axis=0, tiled=True),
        lax.all_gather(word_bias_one, ("dp", "fsdp"), axis=0, tiled=True),
        lax.all_gather(word_inward, ("dp", "fsdp"), axis=0, tiled=True),
        lax.all_gather(word_outward, ("dp", "fsdp"), axis=0, tiled=True),
        lax.all_gather(word_gain_two, ("dp", "fsdp"), axis=0, tiled=True),
        lax.all_gather(word_bias_two, ("dp", "fsdp"), axis=0, tiled=True),
        lax.all_gather(word_expand, ("dp", "fsdp"), axis=0, tiled=True),
        lax.all_gather(word_expand_bias, ("dp", "fsdp"), axis=0, tiled=True),
        lax.all_gather(word_reduce, ("dp", "fsdp"), axis=0, tiled=True),
        lax.all_gather(word_reduce_bias, ("dp", "fsdp"), axis=0, tiled=True),
    )
    row_count, local_words = char_counts.shape
    char_state = char_pass(char_full, char_inputs, language_ids, char_counts)
    word_in = char_state[-1].reshape(row_count, local_words, -1)
    word_state, words_out = word_pass(word_full, word_in, row_lengths)
    grad_word_in, word_grads = word_back(word_full, word_in, word_state, cotangent)
    back_weights = (
        lax.all_gather(language_table, ("dp", "fsdp"), axis=1, tiled=True),
        lax.all_gather(char_gain_one, ("dp", "fsdp"), axis=0, tiled=True),
        lax.all_gather(char_bias_one, ("dp", "fsdp"), axis=0, tiled=True),
        lax.all_gather(char_inward, ("dp", "fsdp"), axis=0, tiled=True),
        lax.all_gather(char_outward, ("dp", "fsdp"), axis=0, tiled=True),
        lax.all_gather(char_gain_two, ("dp", "fsdp"), axis=0, tiled=True),
        lax.all_gather(char_bias_two, ("dp", "fsdp"), axis=0, tiled=True),
        lax.all_gather(char_expand, ("dp", "fsdp"), axis=0, tiled=True),
        lax.all_gather(char_expand_bias, ("dp", "fsdp"), axis=0, tiled=True),
        lax.all_gather(char_reduce, ("dp", "fsdp"), axis=0, tiled=True),
        lax.all_gather(char_reduce_bias, ("dp", "fsdp"), axis=0, tiled=True),
        lax.all_gather(char_to_word, ("dp", "fsdp"), axis=0, tiled=True),
        lax.all_gather(char_to_word_bias, ("dp", "fsdp"), axis=0, tiled=True),
    )
    again_state = char_pass(back_weights, char_inputs, language_ids, char_counts)
    char_input_grad, char_grads = char_back(
        back_weights,
        again_state,
        grad_word_in.reshape(-1, grad_word_in.shape[-1]),
        char_inputs.shape,
    )
    all_shards = (
        lax.psum_scatter(char_grads[0], ("dp", "fsdp"), scatter_dimension=1, tiled=True),
        lax.psum_scatter(char_grads[1], ("dp", "fsdp"), scatter_dimension=0, tiled=True),
        lax.psum_scatter(char_grads[2], ("dp", "fsdp"), scatter_dimension=0, tiled=True),
        lax.psum_scatter(char_grads[3], ("dp", "fsdp"), scatter_dimension=0, tiled=True),
        lax.psum_scatter(char_grads[4], ("dp", "fsdp"), scatter_dimension=0, tiled=True),
        lax.psum_scatter(char_grads[5], ("dp", "fsdp"), scatter_dimension=0, tiled=True),
        lax.psum_scatter(char_grads[6], ("dp", "fsdp"), scatter_dimension=0, tiled=True),
        lax.psum_scatter(char_grads[7], ("dp", "fsdp"), scatter_dimension=0, tiled=True),
        lax.psum_scatter(char_grads[8], ("dp", "fsdp"), scatter_dimension=0, tiled=True),
        lax.psum_scatter(char_grads[9], ("dp", "fsdp"), scatter_dimension=0, tiled=True),
        lax.psum_scatter(char_grads[10], ("dp", "fsdp"), scatter_dimension=0, tiled=True),
        lax.psum_scatter(char_grads[11], ("dp", "fsdp"), scatter_dimension=0, tiled=True),
        lax.psum_scatter(char_grads[12], ("dp", "fsdp"), scatter_dimension=0, tiled=True),
        lax.psum_scatter(word_grads[0], ("dp", "fsdp"), scatter_dimension=0, tiled=True),
        lax.psum_scatter(word_grads[1], ("dp", "fsdp"), scatter_dimension=0, tiled=True),
        lax.psum_scatter(word_grads[2], ("dp", "fsdp"), scatter_dimension=0, tiled=True),
        lax.psum_scatter(word_grads[3], ("dp", "fsdp"), scatter_dimension=0, tiled=True),
        lax.psum_scatter(word_grads[4], ("dp", "fsdp"), scatter_dimension=0, tiled=True),
        lax.psum_scatter(word_grads[5], ("dp", "fsdp"), scatter_dimension=0, tiled=True),
        lax.psum_scatter(word_grads[6], ("dp", "fsdp"), scatter_dimension=0, tiled=True),
        lax.psum_scatter(word_grads[7], ("dp", "fsdp"), scatter_dimension=0, tiled=True),
        lax.psum_scatter(word_grads[8], ("dp", "fsdp"), scatter_dimension=0, tiled=True),
        lax.psum_scatter(word_grads[9], ("dp", "fsdp"), scatter_dimension=0, tiled=True),
    )
    return (words_out, char_input_grad) + tuple(all_shards)


def solution(mesh):
    in_specs = (
        P("dp", "fsdp", None, None),
        P("dp"),
        P("dp", "fsdp"),
        P("dp"),
        P("dp", "fsdp", None),
        P(None, ("dp", "fsdp")),
        P(("dp", "fsdp")),
        P(("dp", "fsdp")),
        P(("dp", "fsdp"), None),
        P(("dp", "fsdp"), None),
        P(("dp", "fsdp")),
        P(("dp", "fsdp")),
        P(("dp", "fsdp"), None),
        P(("dp", "fsdp")),
        P(("dp", "fsdp"), None),
        P(("dp", "fsdp")),
        P(("dp", "fsdp"), None),
        P(("dp", "fsdp")),
        P(("dp", "fsdp")),
        P(("dp", "fsdp")),
        P(("dp", "fsdp"), None),
        P(("dp", "fsdp"), None),
        P(("dp", "fsdp")),
        P(("dp", "fsdp")),
        P(("dp", "fsdp"), None),
        P(("dp", "fsdp")),
        P(("dp", "fsdp"), None),
        P(("dp", "fsdp")),
    )
    out_specs = (
        P("dp", "fsdp", None),
        P("dp", "fsdp", None, None),
        P(None, ("dp", "fsdp")),
        P(("dp", "fsdp")),
        P(("dp", "fsdp")),
        P(("dp", "fsdp"), None),
        P(("dp", "fsdp"), None),
        P(("dp", "fsdp")),
        P(("dp", "fsdp")),
        P(("dp", "fsdp"), None),
        P(("dp", "fsdp")),
        P(("dp", "fsdp"), None),
        P(("dp", "fsdp")),
        P(("dp", "fsdp"), None),
        P(("dp", "fsdp")),
        P(("dp", "fsdp")),
        P(("dp", "fsdp")),
        P(("dp", "fsdp"), None),
        P(("dp", "fsdp"), None),
        P(("dp", "fsdp")),
        P(("dp", "fsdp")),
        P(("dp", "fsdp"), None),
        P(("dp", "fsdp")),
        P(("dp", "fsdp"), None),
        P(("dp", "fsdp")),
    )
    return jax.shard_map(body, mesh=mesh, in_specs=in_specs, out_specs=out_specs, check_vma=False)
```

profile of v0, /device:TPU:0, one launch (start us, length us, event | category | flops | bytes accessed | tf_op | source)
XLA Modules:
  0.0 1902.5 jit_solution(3433058720473235094)
XLA Ops:
  19.0 42.3 %all-reduce.28 = (bf16[512]{0:T(512)(128)(2,1)S(1)}, bf16[256]{0:T(256)(128)(2,1)S(1)}, bf16[256]{0:T(256)(128)(2,1)S(1)}, bf16[256]{0:T(256)(128)(2,1)S(1)}, bf...) all-reduce(bf16[512]{0:T(512)(128)(2,1)S(1)} %dynamic-update-slice., ...), channel_id=1, replica_groups=mesh['dp'=8,'fsdp'=4] {'dp','fsdp'}, use_global_device_ids=true, to_apply=%add.6 | all-reduce | flops 7424 | bytes 29696
  61.3 41.4 %all_gather.84 = bf16[32,256]{0,1:T(8,128)(2,1)S(1)} all-gather(bf16[32,8]{0,1:T(8,128)(2,1)} %param.33), channel_id=1, replica_groups=mesh['dp'=8,'fsdp'=4] {'dp','fsdp'}, dimensions={1}, use_global_device_ids=true | all-gather | bytes 16896 | tf_op jit(solution)/shard_map/all_gather | solution.py:463
  121.0 37.9 %all_gather.87 = bf16[256,768]{1,0:T(8,128)(2,1)S(1)} all-gather(bf16[8,768]{1,0:T(8,128)(2,1)S(1)} %copy-done.61), channel_id=1, replica_groups=mesh['dp'=8,'fsdp'=4] {'dp','fsdp'}, dimensions={0}, use_global_device_ids=true | all-gather | bytes 405504 | tf_op jit(solution)/shard_map/all_gather | solution.py:466
  286.7 38.3 %all_gather.88 = bf16[256,256]{1,0:T(8,128)(2,1)S(1)} all-gather(bf16[8,256]{1,0:T(8,128)(2,1)S(1)} %copy-done.75), channel_id=1, replica_groups=mesh['dp'=8,'fsdp'=4] {'dp','fsdp'}, dimensions={0}, use_global_device_ids=true | all-gather | bytes 135168 | tf_op jit(solution)/shard_map/all_gather | solution.py:467
  335.8 38.0 %all_gather.91 = bf16[256,1024]{1,0:T(8,128)(2,1)S(1)} all-gather(bf16[8,1024]{1,0:T(8,128)(2,1)S(1)} %copy-done.58), channel_id=1, replica_groups=mesh['dp'=8,'fsdp'=4] {'dp','fsdp'}, dimensions={0}, use_global_device_ids=true | all-gather | bytes 540672 | tf_op jit(solution)/shard_map/all_gather | solution.py:470
  373.9 19.4 %multiply_convert_fusion = (bf16[512,16,1024]{2,0,1:T(8,128)(2,1)}, f32[512,16,1024]{2,0,1:T(8,128)}) fusion(f32[1024]{0:T(1024)S(1)} %convert_element_type.205, bf16[256,1024]{1,0:T(8,128)(2,1)S(1)} %all_gather.91, f32[512,16,256]{2,0,1:T(8,128)S(1)} %get-tuple-element.263, f32[256]{0:T(256)S(1)} %convert_element_type.203, ...), kind=kOutput, calls=%fused_computation.12 | convolution fusion | flops 4389339136 | bytes 59316224 | tf_op jit(solution)/shard_map/dot_general | solution.py:16
  393.3 38.7 %all_gather.95 = bf16[256,512]{1,0:T(8,128)(2,1)S(1)} all-gather(bf16[8,512]{1,0:T(8,128)(2,1)S(1)} %copy-done.71), channel_id=1, replica_groups=mesh['dp'=8,'fsdp'=4] {'dp','fsdp'}, dimensions={0}, use_global_device_ids=true | all-gather | bytes 270336 | tf_op jit(solution)/shard_map/all_gather | solution.py:474
  432.0 38.1 %all_gather.93 = bf16[1024,256]{1,0:T(8,128)(2,1)S(1)} all-gather(bf16[32,256]{1,0:T(8,128)(2,1)S(1)} %copy-done.59), channel_id=1, replica_groups=mesh['dp'=8,'fsdp'=4] {'dp','fsdp'}, dimensions={0}, use_global_device_ids=true | all-gather | bytes 540672 | tf_op jit(solution)/shard_map/all_gather | solution.py:472
  485.7 42.6 %all_gather.101 = bf16[512,512]{1,0:T(8,128)(2,1)} all-gather(bf16[16,512]{1,0:T(8,128)(2,1)S(1)} %copy-done.60), channel_id=1, replica_groups=mesh['dp'=8,'fsdp'=4] {'dp','fsdp'}, dimensions={0}, use_global_device_ids=true | all-gather | bytes 540672 | tf_op jit(solution)/shard_map/all_gather | solution.py:481
  561.2 18.2 all-gather.9.cloned.1.call-done
  584.3 53.1 %all-gather.11.cloned.1.call-done = bf16[2048,512]{1,0:T(8,128)(2,1)} async-done(((bf16[64,512]{1,0:T(8,128)(2,1)}), bf16[2048,512]{1,0:T(8,128)(2,1)}) %all-gather.11.cloned.1.call-update) | async-done | bytes 2097168 | tf_op jit(solution)/shard_map/all_gather | solution.py:486
  650.8 14.5 multiply_reduce_fusion
  766.4 31.6 %convert_reduce_fusion = (f32[1024]{0:T(1024)}, bf16[512,16,1024]{2,0,1:T(8,128)(2,1)}) fusion(f32[512,16,1024]{2,0,1:T(8,128)} %get-tuple-element.265, f32[1024]{0:T(1024)S(1)} %convert_element_type.205, bf16[1024,256]{1,0:T(8,128)(2,1)S(1)} %copy-done.38, f32[512,256]{1,0:T(8,128)S(1)} %convolution_divide_fusion, f32[512,16]{0,1:T(8,128)S(1)} %fusion.87), kind=kOutput, calls=%fused_computation.11 | convolution fusion | flops 4492098560 | bytes 51421184 | tf_op jit(solution)/shard_map/dot_general | solution.py:20
  875.2 15.0 copy.328
  906.6 13.6 fusion.19
  920.7 13.5 convert_bitcast_fusion
  1058.9 43.8 %all-reduce.27 = (f32[32,256]{0,1:T(8,128)S(1)}, f32[256]{0:T(256)S(1)}, f32[256]{0:T(256)S(1)}, f32[256]{0:T(256)S(1)}, f32[256]{0:T(256)S(1)}, /*index=5*/f32[...) all-reduce(f32[32,256]{0,1:T(8,128)S(1)} %fusion.90, ...), channel_id=3, replica_groups=mesh['dp'=8,'fsdp'=4] {'dp','fsdp'}, use_global_device_ids=true, to_apply=%region_26.27.clone | all-reduce | flops 15616 | bytes 124928
  1122.6 37.8 %reduce-scatter.29.cloned.1.call-done = f32[64,512]{1,0:T(8,128)} async-done(((f32[2048,512]{1,0:T(8,128)}), f32[64,512]{1,0:T(8,128)}) %reduce-scatter.29.cloned.1.call-update) | async-done | bytes 131088 | tf_op jit(solution)/shard_map/reduce_scatter | solution.py:538
  1160.4 132.1 %reduce-scatter.15.cloned.1.call-done = f32[8,256]{1,0:T(8,128)} async-done(((f32[256,256]{1,0:T(8,128)}), f32[8,256]{1,0:T(8,128)}) %reduce-scatter.15.cloned.1.call-update) | async-done | bytes 8208 | tf_op jit(solution)/shard_map/reduce_scatter | solution.py:521
  1292.6 132.5 %reduce-scatter.21.cloned.1.call-done = f32[8,512]{1,0:T(8,128)} async-done(((f32[256,512]{1,0:T(8,128)}), f32[8,512]{1,0:T(8,128)}) %reduce-scatter.21.cloned.1.call-update) | async-done | bytes 16400 | tf_op jit(solution)/shard_map/reduce_scatter | solution.py:528
  1425.0 97.1 %reduce-scatter.13.cloned.1.call-done = f32[8,768]{1,0:T(8,128)} async-done(((f32[256,768]{1,0:T(8,128)}), f32[8,768]{1,0:T(8,128)}) %reduce-scatter.13.cloned.1.call-update) | async-done | bytes 24592 | tf_op jit(solution)/shard_map/reduce_scatter | solution.py:520
  1522.1 136.5 %reduce-scatter.19.cloned.1.call-done = f32[32,256]{1,0:T(8,128)} async-done(((f32[1024,256]{1,0:T(8,128)}), f32[32,256]{1,0:T(8,128)}) %reduce-scatter.19.cloned.1.call-update) | async-done | bytes 32784 | tf_op jit(solution)/shard_map/reduce_scatter | solution.py:526
  1658.7 133.6 %reduce-scatter.17.cloned.1.call-done = f32[8,1024]{1,0:T(8,128)} async-done(((f32[256,1024]{1,0:T(8,128)}), f32[8,1024]{1,0:T(8,128)}) %reduce-scatter.17.cloned.1.call-update) | async-done | bytes 32784 | tf_op jit(solution)/shard_map/reduce_scatter | solution.py:524
  1792.3 103.4 %reduce-scatter.23.cloned.1.call-done = f32[16,1536]{1,0:T(8,128)} async-done(((f32[512,1536]{1,0:T(8,128)}), f32[16,1536]{1,0:T(8,128)}) %reduce-scatter.23.cloned.1.call-update) | async-done | bytes 98320 | tf_op jit(solution)/shard_map/reduce_scatter | solution.py:532
  (413 shorter events, 573.8 us)
Async XLA Ops:
  7.2 473.1 %all-gather.5.cloned.1.call-start = ((), (), s32[]{:S(2)}) async-start(), calls=%async_computation.10 | async-start | bytes 1622016 | tf_op jit(solution)/shard_map/all_gather | solution.py:480
  7.9 522.4 %all-gather.7.cloned.1.call-start = ((), (), s32[]{:S(2)}) async-start(), calls=%async_computation.11 | async-start | bytes 5242880 | tf_op jit(solution)/shard_map/all_gather | solution.py:279
  61.3 97.6 %copy-start.66 = (f32[256]{0:T(256)}, f32[256]{0:T(256)S(1)}, u32[]{:S(2)}) copy-start(f32[256]{0:T(256)S(1)} %convert_element_type.194) | copy-start | bytes 3076
  332.4 137.7 %copy-start.1 = (f32[512,16,256]{2,0,1:T(8,128)}, f32[512,16,256]{2,0,1:T(8,128)S(1)}, u32[]{:S(2)}) copy-start(f32[512,16,256]{2,0,1:T(8,128)S(1)} %get-tuple-element.263) | copy-start | bytes 25165828
  432.0 333.6 %copy-start.84 = (f32[512]{0:T(512)}, f32[512]{0:T(512)S(1)}, u32[]{:S(2)}) copy-start(f32[512]{0:T(512)S(1)} %convert_element_type.209) | copy-start | bytes 6148
  479.9 284.1 %copy-start.5 = (f32[512,512]{1,0:T(8,128)}, f32[512,512]{1,0:T(8,128)S(1)}, u32[]{:S(2)}) copy-start(f32[512,512]{1,0:T(8,128)S(1)} %get-tuple-element.267) | copy-start | bytes 3145732
  479.9 284.1 %copy-start.50 = (f32[2,256]{1,0:T(2,128)}, f32[2,256]{1,0:T(2,128)S(1)}, u32[]{:S(2)}) copy-start(f32[2,256]{1,0:T(2,128)S(1)} %div.136) | copy-start | bytes 6148
  480.2 283.8 %copy-start.52 = (f32[2,256]{1,0:T(2,128)}, f32[2,256]{1,0:T(2,128)S(1)}, u32[]{:S(2)}) copy-start(f32[2,256]{1,0:T(2,128)S(1)} %rsqrt.48) | copy-start | bytes 6148
  480.3 283.8 %copy-start.54 = (f32[512]{0:T(512)}, f32[512]{0:T(512)S(1)}, u32[]{:S(2)}) copy-start(f32[512]{0:T(512)S(1)} %convert_element_type.212) | copy-start | bytes 6148
  483.9 95.5 %all-gather.9.cloned.1.call-start = ((), (), s32[]{:S(2)}) async-start(), calls=%async_computation.12 | async-start | bytes 2162688 | tf_op jit(solution)/shard_map/all_gather | solution.py:484
  484.7 152.8 %all-gather.11.cloned.1.call-start = ((), (), s32[]{:S(2)}) async-start(), calls=%async_computation.13 | async-start | bytes 2162688 | tf_op jit(solution)/shard_map/all_gather | solution.py:486
  485.2 273.9 %reduce-scatter.11.cloned.1.call-start = ((), (), s32[]{:S(2)}) async-start(), calls=%async_computation.14 | async-start | bytes 5242880 | tf_op jit(solution)/shard_map/reduce_scatter | solution.py:404
  485.7 278.3 %copy-start.64 = (pred[2,256]{1,0:T(4,128)(4,1)}, pred[2,256]{1,0:T(4,128)(4,1)S(1)}, u32[]{:S(2)}) copy-start(pred[2,256]{1,0:T(4,128)(4,1)S(1)} %broadcast_compare_fusion) | copy-start | bytes 1540
  528.3 224.5 %copy-start.73 = (f32[2048]{0:T(1024)}, f32[2048]{0:T(1024)S(1)}, u32[]{:S(2)}) copy-start(f32[2048]{0:T(1024)S(1)} %convert_element_type.223) | copy-start | bytes 24580
  560.9 139.8 %copy-start.7 = (f32[2,256,512]{2,1,0:T(8,128)}, f32[2,256,512]{2,1,0:T(8,128)S(1)}, u32[]{:S(2)}) copy-start(f32[2,256,512]{2,1,0:T(8,128)S(1)} %get-tuple-element.271) | copy-start | bytes 3145732
  699.1 423.5 %reduce-scatter.25.cloned.1.call-start = ((), (), s32[]{:S(2)}) async-start(), calls=%async_computation.21 | async-start | bytes 1081344 | tf_op jit(solution)/shard_map/reduce_scatter | solution.py:533
  700.6 422.0 %reduce-scatter.27.cloned.1.call-start = ((), (), s32[]{:S(2)}) async-start(), calls=%async_computation.22 | async-start | bytes 4325376 | tf_op jit(solution)/shard_map/reduce_scatter | solution.py:536
  705.7 454.7 %reduce-scatter.29.cloned.1.call-start = ((), (), s32[]{:S(2)}) async-start(), calls=%async_computation.23 | async-start | bytes 4325376 | tf_op jit(solution)/shard_map/reduce_scatter | solution.py:538
  759.1 533.5 %reduce-scatter.15.cloned.1.call-start = ((), (), s32[]{:S(2)}) async-start(), calls=%async_computation.16 | async-start | bytes 270336 | tf_op jit(solution)/shard_map/reduce_scatter | solution.py:521
  920.3 504.8 %reduce-scatter.21.cloned.1.call-start = ((), (), s32[]{:S(2)}) async-start(), calls=%async_computation.19 | async-start | bytes 540672 | tf_op jit(solution)/shard_map/reduce_scatter | solution.py:528
  984.0 538.1 %reduce-scatter.13.cloned.1.call-start = ((), (), s32[]{:S(2)}) async-start(), calls=%async_computation.15 | async-start | bytes 811008 | tf_op jit(solution)/shard_map/reduce_scatter | solution.py:520
  992.9 665.7 %reduce-scatter.19.cloned.1.call-start = ((), (), s32[]{:S(2)}) async-start(), calls=%async_computation.18 | async-start | bytes 1081344 | tf_op jit(solution)/shard_map/reduce_scatter | solution.py:526
  1005.9 786.4 %reduce-scatter.17.cloned.1.call-start = ((), (), s32[]{:S(2)}) async-start(), calls=%async_computation.17 | async-start | bytes 1081344 | tf_op jit(solution)/shard_map/reduce_scatter | solution.py:524
  1018.9 876.7 %reduce-scatter.23.cloned.1.call-start = ((), (), s32[]{:S(2)}) async-start(), calls=%async_computation.20 | async-start | bytes 3244032 | tf_op jit(solution)/shard_map/reduce_scatter | solution.py:532
  (90 other events, 1345.4 us)
Sparse Core Ops, SparseCore 0:
  10.9 58.0 all-gather.4
  484.1 36.1 all-gather.6
  523.1 56.2 all-gather.8
  582.1 55.2 all-gather.10
  699.2 43.3 reduce-scatter.10
  745.4 134.7 reduce-scatter.24
  883.1 137.2 reduce-scatter.26
  1023.2 137.2 reduce-scatter.28
  1163.3 129.2 reduce-scatter.14
  1295.3 129.6 reduce-scatter.20
  1430.7 91.3 reduce-scatter.12
  1524.8 133.8 reduce-scatter.18
  1661.6 130.6 reduce-scatter.16
  1798.2 97.4 reduce-scatter.22
where the time goes:
time: 1920 us; the launch traced here: 1900 us
  waiting for transfers between devices  847 us (44%)
  blocking collectives  361 us (19%)
  matrix products  306 us (16%)
  local copies, waits for them, and re-layouts  302 us (16%)
  other arithmetic  69.8 us (4%)
    reduce_scatter x1, waiting for transfers between devices, body(): lax.psum_scatter(char_grads[9], ('dp', 'fsdp'), scatter_dimension=0, tile...  137 us
    reduce_scatter x1, waiting for transfers between devices, body(): lax.psum_scatter(char_grads[7], ('dp', 'fsdp'), scatter_dimension=0, tile...  134 us
    reduce_scatter x1, waiting for transfers between devices, body(): lax.psum_scatter(char_grads[11], ('dp', 'fsdp'), scatter_dimension=0, til...  132 us
    reduce_scatter x1, waiting for transfers between devices, body(): lax.psum_scatter(char_grads[4], ('dp', 'fsdp'), scatter_dimension=0, tile...  132 us
    reduce_scatter x1, waiting for transfers between devices, body(): lax.psum_scatter(word_grads[2], ('dp', 'fsdp'), scatter_dimension=0, tile...  103 us
    reduce_scatter x1, waiting for transfers between devices, body(): lax.psum_scatter(char_grads[3], ('dp', 'fsdp'), scatter_dimension=0, tile...  97.1 us
    unnamed x2, blocking collectives  86.1 us
    dot_general x9, matrix products, back_product(): lax.dot_general(grad_low, weight, (((grad_low.ndim - 1,), (1,)), ((), ())...  74.7 us
  transfers between devices with their start and end apart: 14, of which 9 were waited for; matrix products, arithmetic and copies ran while one was open for 32% of the time, Pallas kernels for 0%

commit v1 on v0

v1 whole, which is shorter than its diff:
```python
import functools

import jax
import jax.numpy as jnp
from jax import lax
from jax.experimental import pallas as pl
from jax.experimental.pallas import tpu as pltpu
from jax.sharding import PartitionSpec as P

BF = jnp.bfloat16
F32 = jnp.float32
EPS = 1e-05
MASKED = -1e30
CHEADS = 4
WHEADS = 8
HEAD = 64
SCALE = HEAD ** (-0.5)
GROUP = 128
BLOCK = 512
SPLIT = BLOCK // GROUP
FOLD = 4
SMALL = 128
GELU_A = 0.7978845608028654
GELU_B = 0.044715
MIB = 1024 * 1024


def dot(a, b):
    return jnp.dot(a, b, preferred_element_type=F32)


def dot_t(a, b):
    return lax.dot_general(a, b, (((1,), (1,)), ((), ())), preferred_element_type=F32)


def t_dot(a, b):
    return lax.dot_general(a, b, (((0,), (0,)), ((), ())), preferred_element_type=F32)


def norm_parts(hidden):
    centred = hidden - jnp.mean(hidden, -1, keepdims=True)
    spread = lax.rsqrt(jnp.mean(centred * centred, -1, keepdims=True) + EPS)
    return centred * spread, spread


def norm_back(unit, spread, gained):
    return (
        gained
        - jnp.mean(gained, -1, keepdims=True)
        - unit * jnp.mean(gained * unit, -1, keepdims=True)
    ) * spread


def gelu_both(pre):
    square = pre * pre
    turn = jnp.tanh(pre * (GELU_A + (GELU_A * GELU_B) * square))
    half = 0.5 + 0.5 * turn
    slope = half + pre * half * (1.0 - turn) * (GELU_A + (3.0 * GELU_A * GELU_B) * square)
    return pre * half, slope


def fold_rows(values):
    rows, width = values.shape
    return jnp.sum(values.reshape(rows // 8, 8, width), 0)


def head_masks(width, heads):
    lanes = lax.broadcasted_iota(jnp.int32, (1, width), 1) // HEAD
    return [(lanes == h).astype(F32).astype(BF) for h in range(heads)]


def live_steps(kernel):
    def run(settings, blocks, *refs):
        @pl.when(pl.program_id(0) < blocks[0])
        def _():
            kernel(settings, blocks, *refs)

    return run


def full(shape):
    return pl.BlockSpec(shape, lambda *_: (0,) * len(shape))


def pack_kernel(
    per_row, counts, chars, packed, bias, hot, offs, first, rows_of, blocks, tags, *wide
):
    words, slots, width = chars.shape
    for part in wide:
        part[...] = jnp.zeros_like(part)
    tags[...] = jnp.full_like(tags, -1.0)

    def clear(g, carry):
        first[g] = 0
        rows_of[g] = 0
        return carry

    lax.fori_loop(0, first.shape[0], clear, 0)
    slot = lax.broadcasted_iota(jnp.int32, (slots, GROUP), 0)

    def place(w, at):
        live = counts[w]
        inside = lax.rem(at, GROUP)
        fresh = (inside + live > GROUP) | (lax.rem(w, per_row) == 0)
        at = jnp.where(fresh, lax.div(at + (GROUP - 1), GROUP) * GROUP, at)

        @pl.when(lax.rem(at, GROUP) == 0)
        def _():
            first[lax.div(at, GROUP)] = w
            rows_of[lax.div(at, GROUP)] = lax.div(w, per_row)

        for k, part in enumerate(wide):
            part[pl.ds(at, slots), :] = chars[w, :, k * GROUP : (k + 1) * GROUP].astype(F32)
        tags[pl.ds(at, slots), :] = jnp.where(slot < live, w.astype(F32), -1.0)
        offs[w] = at
        return at + live

    end = lax.fori_loop(0, words, place, 0)
    used = lax.div(end + (BLOCK - 1), BLOCK)
    blocks[0] = used
    lane = lax.broadcasted_iota(jnp.int32, (GROUP, GROUP), 1).astype(F32)

    def finish(g, carry):
        here = pl.ds(pl.multiple_of(g * GROUP, GROUP), GROUP)
        tag = tags[here, :]
        bias[here, :] = jnp.where(tag == tag.T, 0.0, MASKED).astype(BF)
        hot[here, :] = (tag - first[g].astype(F32) == lane).astype(F32).astype(BF)
        for k, part in enumerate(wide):
            packed[here, k * GROUP : (k + 1) * GROUP] = part[here, :].astype(BF)
        return carry

    lax.fori_loop(0, used * SPLIT, finish, 0)


def pack(counts, chars, per_row):
    words, slots, width = chars.shape
    groups = (words * slots) // (GROUP - slots + 1) + 1 + words // per_row
    groups = -(-groups // SPLIT) * SPLIT
    rows = groups * GROUP
    smem = pl.BlockSpec(memory_space=pltpu.SMEM)
    vmem = pl.BlockSpec(memory_space=pltpu.VMEM)
    return pl.pallas_call(
        functools.partial(pack_kernel, per_row),
        out_shape=(
            jax.ShapeDtypeStruct((rows, width), BF),
            jax.ShapeDtypeStruct((rows, GROUP), BF),
            jax.ShapeDtypeStruct((rows, GROUP), BF),
            jax.ShapeDtypeStruct((words,), jnp.int32),
            jax.ShapeDtypeStruct((groups,), jnp.int32),
            jax.ShapeDtypeStruct((groups,), jnp.int32),
            jax.ShapeDtypeStruct((1,), jnp.int32),
        ),
        in_specs=[smem, vmem],
        out_specs=(vmem, vmem, vmem, smem, smem, smem, smem),
        scratch_shapes=[pltpu.VMEM((rows + slots, GROUP), F32)] * (1 + width // GROUP),
        compiler_params=pltpu.CompilerParams(vmem_limit_bytes=48 * MIB),
        cost_estimate=pl.CostEstimate(
            flops=rows * width * 4, bytes_accessed=rows * width * 6, transcendentals=0
        ),
    )(counts, chars)


def unpack_kernel(offs, counts, *refs):
    packed, out = refs[:-1], refs[-1]
    here = pl.program_id(0) * out.shape[0]
    slots = out.shape[1]
    slot = lax.broadcasted_iota(jnp.int32, (slots, GROUP), 0)

    def take(k, carry):
        w = here + k
        for j, part in enumerate(packed):
            rows = part[pl.ds(offs[w], slots), :]
            out[k, :, j * GROUP : (j + 1) * GROUP] = jnp.where(slot < counts[w], rows, 0.0)
        return carry

    lax.fori_loop(0, out.shape[0], take, 0)


def unpack(offs, counts, packed, words, slots):
    width = len(packed) * GROUP
    step = words // 8
    return pl.pallas_call(
        unpack_kernel,
        out_shape=jax.ShapeDtypeStruct((words, slots, width), F32),
        grid_spec=pltpu.PrefetchScalarGridSpec(
            num_scalar_prefetch=2,
            grid=(words // step,),
            in_specs=[full(part.shape) for part in packed],
            out_specs=pl.BlockSpec((step, slots, width), lambda i, *_: (i, 0, 0)),
        ),
        compiler_params=pltpu.CompilerParams(vmem_limit_bytes=48 * MIB),
        cost_estimate=pl.CostEstimate(
            flops=words * slots * width, bytes_accessed=words * slots * width * 8, transcendentals=0
        ),
    )(offs, counts, *packed)


def with_language(i, rows_of, ids, packed, small_rows):
    parts = []
    for g in range(SPLIT):
        row = small_rows[pl.ds(ids[rows_of[i * SPLIT + g]], 1), :]
        parts.append(packed[g * GROUP : (g + 1) * GROUP, :].astype(F32) + row)
    return jnp.concatenate(parts, 0)


def stack_heads(values, masks):
    return jnp.concatenate([values * mask for mask in masks], 0)


@live_steps
def char_attend_kernel(
    langs,
    blocks,
    rows_of, ids, packed, bias, weights, qkv_out, soft_out, mixed_out, after_out, small_rows
):
    i = pl.program_id(0)
    width = packed.shape[1]

    @pl.when(i == 0)
    def _():
        small_rows[...] = weights[:, 4 * width :].astype(F32).T

    start = with_language(i, rows_of, ids, packed, small_rows)
    unit, _ = norm_parts(start)
    normed = (unit * small_rows[langs : langs + 1, :] + small_rows[langs + 1 : langs + 2, :]).astype(BF)
    qkv_out[...] = dot(normed, weights[:, : 3 * width]).astype(BF)
    masks = head_masks(width, CHEADS)
    for g in range(SPLIT):
        here = slice(g * GROUP, (g + 1) * GROUP)
        keys = stack_heads(qkv_out[here, width : 2 * width], masks)
        scores = dot_t(qkv_out[here, :width], keys) * SCALE
        blocked = bias[here, :].astype(F32)
        parts = []
        for h in range(CHEADS):
            one = scores[:, h * GROUP : (h + 1) * GROUP] + blocked
            one = jnp.exp(one - jnp.max(one, -1, keepdims=True))
            parts.append((one * (1.0 / jnp.sum(one, -1, keepdims=True))).astype(BF))
        soft = jnp.concatenate(parts, 1)
        soft_out[here, :] = soft
        values = stack_heads(qkv_out[here, 2 * width :], masks)
        mixed_out[here, :] = dot(soft, values).astype(BF)
    after_out[...] = start + dot(mixed_out[...], weights[:, 3 * width : 4 * width])


@live_steps
def char_ffn_kernel(
    langs,
    blocks,
    first, after, hot, inverse, small, weights, act_out, slope_out, pooled_out, small_rows, *total
):
    i = pl.program_id(0)
    width = after.shape[1]
    hidden = FOLD * width

    @pl.when(i == 0)
    def _():
        small_rows[...] = small[...].astype(F32).T
        for part in total:
            part[...] = jnp.zeros_like(part)

    unit, _ = norm_parts(after[...])
    normed = (unit * small_rows[langs + 2 : langs + 3, :] + small_rows[langs + 3 : langs + 4, :]).astype(BF)
    out = after[...] + small_rows[langs + 4 : langs + 5, :]
    for j in range(FOLD):
        cols = slice(j * width, (j + 1) * width)
        pre = dot(normed, weights[:, cols]) + small_rows[langs + 5 + j : langs + 6 + j, :]
        act, slope = gelu_both(pre)
        act = act.astype(BF)
        act_out[:, cols] = act
        slope_out[:, cols] = slope.astype(BF)
        out = out + dot(act, weights[:, hidden + j * width : hidden + (j + 1) * width])
    out = out.astype(BF)
    for g in range(SPLIT):
        here = slice(g * GROUP, (g + 1) * GROUP)
        words = pl.ds(first[i * SPLIT + g], GROUP)
        found = t_dot(hot[here, :], out[here, :])
        for k, part in enumerate(total):
            part[words, :] = part[words, :] + found[:, k * GROUP : (k + 1) * GROUP]

    @pl.when(i == blocks[0] - 1)
    def _():
        for k, part in enumerate(total):
            pooled_out[:, k * GROUP : (k + 1) * GROUP] = (
                part[: pooled_out.shape[0], :] * inverse[...]
            ).astype(BF)


def rows_spec(width):
    return pl.BlockSpec((BLOCK, width), lambda i, blocks, *_: (jnp.minimum(i, blocks[0] - 1), 0))


def char_attend(langs, blocks, rows_of, ids, packed, bias, weights):
    rows, width = packed.shape
    return pl.pallas_call(
        functools.partial(char_attend_kernel, langs),
        out_shape=(
            jax.ShapeDtypeStruct((rows, 3 * width), BF),
            jax.ShapeDtypeStruct((rows, CHEADS * GROUP), BF),
            jax.ShapeDtypeStruct((rows, width), BF),
            jax.ShapeDtypeStruct((rows, width), F32),
        ),
        grid_spec=pltpu.PrefetchScalarGridSpec(
            num_scalar_prefetch=3,
            grid=(rows // BLOCK,),
            in_specs=[rows_spec(width), rows_spec(GROUP), full(weights.shape)],
            out_specs=(
                rows_spec(3 * width),
                rows_spec(CHEADS * GROUP),
                rows_spec(width),
                rows_spec(width),
            ),
            scratch_shapes=[pltpu.VMEM((SMALL, width), F32)],
        ),
        compiler_params=pltpu.CompilerParams(vmem_limit_bytes=48 * MIB),
        cost_estimate=pl.CostEstimate(
            flops=rows * width * width * 12, bytes_accessed=rows * width * 12, transcendentals=rows * 512
        ),
    )(blocks, rows_of, ids, packed, bias, weights)


def char_ffn(langs, blocks, first, after, hot, inverse, small_of, weights):
    rows, width = after.shape
    words = inverse.shape[0]
    hidden = FOLD * width
    return pl.pallas_call(
        functools.partial(char_ffn_kernel, langs),
        out_shape=(
            jax.ShapeDtypeStruct((rows, hidden), BF),
            jax.ShapeDtypeStruct((rows, hidden), BF),
            jax.ShapeDtypeStruct((words, width), BF),
        ),
        grid_spec=pltpu.PrefetchScalarGridSpec(
            num_scalar_prefetch=2,
            grid=(rows // BLOCK,),
            in_specs=[
                rows_spec(width),
                rows_spec(GROUP),
                full(inverse.shape),
                pl.BlockSpec((width, SMALL), lambda i, *_: (0, 4 * width // SMALL)),
                full(weights.shape),
            ],
            out_specs=(rows_spec(hidden), rows_spec(hidden), full((words, width))),
            scratch_shapes=[pltpu.VMEM((SMALL, width), F32)]
            + [pltpu.VMEM((words + GROUP, GROUP), F32)] * (width // GROUP),
        ),
        compiler_params=pltpu.CompilerParams(vmem_limit_bytes=48 * MIB),
        cost_estimate=pl.CostEstimate(
            flops=rows * width * width * 16, bytes_accessed=rows * width * 20, transcendentals=rows * 1024
        ),
    )(blocks, first, after, hot, inverse, small_of, weights)


@live_steps
def char_ffn_back_kernel(
    langs,
    blocks,
    first,
    after,
    hot,
    act,
    slope,
    inverse,
    upstream,
    small,
    weights,
    grad_to_word,
    grad_after,
    grads,
    sums_out,
    small_rows,
    grad_expand,
    grad_reduce,
    sums,
    up_rows,
    *spread_up,
):
    i = pl.program_id(0)
    width = after.shape[1]
    hidden = FOLD * width
    words = upstream.shape[0]

    @pl.when(i == 0)
    def _():
        small_rows[...] = small[...].astype(F32).T
        for k, part in enumerate(spread_up):
            cols = slice(k * GROUP, (k + 1) * GROUP)
            part[:words, :] = upstream[:, cols].astype(F32) * inverse[...]
            part[words:, :] = jnp.zeros((GROUP, GROUP), F32)
        grad_expand[...] = jnp.zeros_like(grad_expand)
        grad_reduce[...] = jnp.zeros_like(grad_reduce)
        sums[...] = jnp.zeros_like(sums)

    for g in range(SPLIT):
        here = slice(g * GROUP, (g + 1) * GROUP)
        for k, part in enumerate(spread_up):
            words_here = part[pl.ds(first[i * SPLIT + g], GROUP), :].astype(BF)
            up_rows[here, k * GROUP : (k + 1) * GROUP] = dot(hot[here, :], words_here).astype(BF)
    up = up_rows[...]
    unit, spread = norm_parts(after[...])
    gain = small_rows[langs + 2 : langs + 3, :]
    normed = (unit * gain + small_rows[langs + 3 : langs + 4, :]).astype(BF)
    grad_normed = jnp.zeros((BLOCK, width), F32)
    for j in range(FOLD):
        cols = slice(j * width, (j + 1) * width)
        grad_act = dot_t(up, weights[:, hidden + j * width : hidden + (j + 1) * width])
        grad_pre = grad_act * slope[:, cols].astype(F32)
        sums[8 * j : 8 * j + 8, :] += fold_rows(grad_pre)
        grad_pre = grad_pre.astype(BF)
        grad_normed = grad_normed + dot_t(grad_pre, weights[:, cols])
        grad_expand[:, cols] += t_dot(normed, grad_pre)
        grad_reduce[:, cols] += t_dot(up, act[:, cols])
    up_wide = up.astype(F32)
    sums[32:40, :] += fold_rows(grad_normed * unit)
    sums[40:48, :] += fold_rows(grad_normed)
    sums[48:56, :] += fold_rows(up_wide)
    grad_after[...] = up_wide + norm_back(unit, spread, grad_normed * gain)

    @pl.when(i == blocks[0] - 1)
    def _():
        grads[:, :hidden] = grad_expand[...].astype(BF)
        for j in range(FOLD):
            grads[:, hidden + j * width : hidden + (j + 1) * width] = (
                grad_reduce[:, j * width : (j + 1) * width].T.astype(BF)
            )
        grads[:, 2 * hidden :] = grad_to_word[...]
        sums_out[...] = sums[...]


def char_ffn_back(
    langs, blocks, first, after, hot, act, slope, inverse, upstream, small_of, weights, grad_to_word
):
    rows, width = after.shape
    words = inverse.shape[0]
    hidden = FOLD * width
    return pl.pallas_call(
        functools.partial(char_ffn_back_kernel, langs),
        out_shape=(
            jax.ShapeDtypeStruct((rows, width), F32),
            jax.ShapeDtypeStruct(weights.shape, BF),
            jax.ShapeDtypeStruct((64, width), F32),
        ),
        grid_spec=pltpu.PrefetchScalarGridSpec(
            num_scalar_prefetch=2,
            grid=(rows // BLOCK,),
            in_specs=[
                rows_spec(width),
                rows_spec(GROUP),
                rows_spec(hidden),
                rows_spec(hidden),
                full(inverse.shape),
                full(upstream.shape),
                pl.BlockSpec((width, SMALL), lambda i, *_: (0, 4 * width // SMALL)),
                full(weights.shape),
                full(grad_to_word.shape),
            ],
            out_specs=(rows_spec(width), full(weights.shape), full((64, width))),
            scratch_shapes=[
                pltpu.VMEM((SMALL, width), F32),
                pltpu.VMEM((width, hidden), F32),
                pltpu.VMEM((width, hidden), F32),
                pltpu.VMEM((64, width), F32),
                pltpu.VMEM((BLOCK, width), BF),
            ]
            + [pltpu.VMEM((words + GROUP, GROUP), F32)] * (width // GROUP),
        ),
        compiler_params=pltpu.CompilerParams(vmem_limit_bytes=48 * MIB),
        cost_estimate=pl.CostEstimate(
            flops=rows * width * width * 32, bytes_accessed=rows * width * 20, transcendentals=0
        ),
    )(blocks, first, after, hot, act, slope, inverse, upstream, small_of, weights, grad_to_word)


@live_steps
def char_attend_back_kernel(
    langs,
    blocks,
    rows_of,
    ids,
    packed,
    qkv,
    soft,
    mixed,
    grad_after,
    weights,
    sums_in,
    grads,
    *refs,
):
    i = pl.program_id(0)
    width = packed.shape[1]
    grad_start = refs[: width // GROUP]
    small_rows, grad_in, grad_out, sums, small_grads, grad_mixed, grad_qkv = refs[width // GROUP :]

    @pl.when(i == 0)
    def _():
        small_rows[...] = weights[:, 4 * width :].astype(F32).T
        grad_in[...] = jnp.zeros_like(grad_in)
        grad_out[...] = jnp.zeros_like(grad_out)
        sums[...] = jnp.zeros_like(sums)
        small_grads[...] = jnp.zeros_like(small_grads)

    start = with_language(i, rows_of, ids, packed, small_rows)
    unit, spread = norm_parts(start)
    gain = small_rows[langs : langs + 1, :]
    normed = (unit * gain + small_rows[langs + 1 : langs + 2, :]).astype(BF)
    after_low = grad_after[...].astype(BF)
    grad_out[...] += t_dot(mixed[...], after_low)
    grad_mixed[...] = dot_t(after_low, weights[:, 3 * width : 4 * width]).astype(BF)
    masks = head_masks(width, CHEADS)
    for g in range(SPLIT):
        here = slice(g * GROUP, (g + 1) * GROUP)
        low = grad_mixed[here, :]
        queries = qkv[here, :width]
        keys = stack_heads(qkv[here, width : 2 * width], masks)
        values = stack_heads(qkv[here, 2 * width :], masks)
        grad_soft = dot_t(low, values)
        parts = []
        grad_keys = jnp.zeros((GROUP, width), F32)
        grad_values = jnp.zeros((GROUP, width), F32)
        for h in range(CHEADS):
            cols = slice(h * GROUP, (h + 1) * GROUP)
            weight = soft[here, cols]
            wide = weight.astype(F32)
            one = grad_soft[:, cols]
            one = wide * (one - jnp.sum(wide * one, -1, keepdims=True))
            one = one.astype(BF)
            parts.append(one)
            grad_keys = grad_keys + t_dot(one, queries * masks[h])
            grad_values = grad_values + t_dot(weight, low * masks[h])
        grad_queries = dot(jnp.concatenate(parts, 1), keys)
        grad_qkv[here, :width] = (grad_queries * SCALE).astype(BF)
        grad_qkv[here, width : 2 * width] = (grad_keys * SCALE).astype(BF)
        grad_qkv[here, 2 * width :] = grad_values.astype(BF)
    grad_in[...] += t_dot(normed, grad_qkv[...])
    grad_normed = dot_t(grad_qkv[...], weights[:, : 3 * width])
    sums[0:8, :] += fold_rows(grad_normed * unit)
    sums[8:16, :] += fold_rows(grad_normed)
    result = grad_after[...] + norm_back(unit, spread, grad_normed * gain)
    for k, part in enumerate(grad_start):
        part[...] = result[:, k * GROUP : (k + 1) * GROUP]
    for g in range(SPLIT):
        line = pl.ds(ids[rows_of[i * SPLIT + g]], 1)
        part = jnp.sum(result[g * GROUP : (g + 1) * GROUP, :], 0, keepdims=True)
        small_grads[line, :] = small_grads[line, :] + part

    @pl.when(i == blocks[0] - 1)
    def _():
        def put(at, block):
            small_grads[langs + at : langs + at + 1, :] = jnp.sum(block, 0, keepdims=True)

        put(0, sums[0:8, :])
        put(1, sums[8:16, :])
        put(2, sums_in[32:40, :])
        put(3, sums_in[40:48, :])
        put(4, sums_in[48:56, :])
        for j in range(FOLD):
            put(5 + j, sums_in[8 * j : 8 * j + 8, :])
        grads[:, : 3 * width] = grad_in[...].astype(BF)
        grads[:, 3 * width : 4 * width] = grad_out[...].astype(BF)
        grads[:, 4 * width :] = small_grads[...].T.astype(BF)


def char_attend_back(langs, blocks, rows_of, ids, packed, qkv, soft, mixed, grad_after, weights, sums):
    rows, width = packed.shape
    return pl.pallas_call(
        functools.partial(char_attend_back_kernel, langs),
        out_shape=(
            jax.ShapeDtypeStruct(weights.shape, BF),
        )
        + (jax.ShapeDtypeStruct((rows + GROUP, GROUP), F32),) * (width // GROUP),
        grid_spec=pltpu.PrefetchScalarGridSpec(
            num_scalar_prefetch=3,
            grid=(rows // BLOCK,),
            in_specs=[
                rows_spec(width),
                rows_spec(3 * width),
                rows_spec(CHEADS * GROUP),
                rows_spec(width),
                rows_spec(width),
                full(weights.shape),
                full(sums.shape),
            ],
            out_specs=(full(weights.shape),) + (rows_spec(GROUP),) * (width // GROUP),
            scratch_shapes=[
                pltpu.VMEM((SMALL, width), F32),
                pltpu.VMEM((width, 3 * width), F32),
                pltpu.VMEM((width, width), F32),
                pltpu.VMEM((16, width), F32),
                pltpu.VMEM((SMALL, width), F32),
                pltpu.VMEM((BLOCK, width), BF),
                pltpu.VMEM((BLOCK, 3 * width), BF),
            ],
        ),
        compiler_params=pltpu.CompilerParams(vmem_limit_bytes=48 * MIB),
        cost_estimate=pl.CostEstimate(
            flops=rows * width * width * 24, bytes_accessed=rows * width * 20, transcendentals=0
        ),
    )(blocks, rows_of, ids, packed, qkv, soft, mixed, grad_after, weights, sums)


def word_kernel(
    place,
    pooled,
    to_word,
    weights,
    cotangent,
    words_out,
    grad_after_out,
    grad_query_out,
    grad_pair_out,
    normed_out,
    word_in_out,
    grads,
    sums_out,
    small_rows,
    word_all,
    normed_all,
    pair,
    query,
    blocked,
    soft_near,
    soft_far,
    mixed,
    after,
    unit_two,
    normed_two,
    up_low,
    total,
    grad_normed,
):
    member = place[0]
    length = place[1]
    all_words, _ = pooled.shape
    width = to_word.shape[1]
    own_words = cotangent.shape[0]
    local = own_words // 2
    half = all_words // 2
    hidden = FOLD * width
    reach = (half, all_words)
    at_in, at_out, at_expand, at_reduce = 0, 3 * width, 4 * width, 4 * width + hidden
    small_rows[...] = weights[:, 4 * width + 2 * hidden :].astype(F32).T

    def embed(t, carry):
        here = pl.ds(pl.multiple_of(t * local, local), local)
        value = dot(pooled[here, :], to_word[...]) + small_rows[5:6, :]
        word_all[here, :] = value
        unit, _ = norm_parts(value)
        normed = (unit * small_rows[0:1, :] + small_rows[1:2, :]).astype(BF)
        normed_all[here, :] = normed
        pair[here, :] = dot(normed, weights[:, width : 3 * width]).astype(BF)
        return carry

    lax.fori_loop(0, all_words // local, embed, 0)
    origin = []
    for t in range(2):
        base = pl.multiple_of(member * local + t * half, local)
        origin.append(base)
        here = slice(t * local, (t + 1) * local)
        word_in_out[here, :] = word_all[pl.ds(base, local), :]
        normed_out[here, :] = normed_all[pl.ds(base, local), :]
    query[...] = dot(normed_out[...], weights[:, :width]).astype(BF)
    masks = head_masks(GROUP, 2)
    softs = (soft_near, soft_far)

    for t in range(2):
        here = slice(t * local, (t + 1) * local)
        keys_seen = reach[t]
        seen = lax.broadcasted_iota(jnp.int32, (local, keys_seen), 1)
        asks = lax.broadcasted_iota(jnp.int32, (local, keys_seen), 0) + origin[t]
        blocked[:, :keys_seen] = jnp.where((seen <= asks) & (seen < length), 0.0, MASKED)

        def attend(p, carry):
            lanes = pl.ds(pl.multiple_of(p * GROUP, GROUP), GROUP)
            after_lanes = pl.ds(pl.multiple_of(width + p * GROUP, GROUP), GROUP)
            asking = query[here, lanes]
            keys = pair[:keys_seen, lanes]
            values = pair[:keys_seen, after_lanes]
            out = jnp.zeros((local, GROUP), F32)
            for h in range(2):
                scores = dot_t(asking * masks[h], keys) * SCALE + blocked[:, :keys_seen]
                scores = jnp.exp(scores - jnp.max(scores, -1, keepdims=True))
                soft = (scores * (1.0 / jnp.sum(scores, -1, keepdims=True))).astype(BF)
                softs[t][2 * p + h] = soft
                out = out + dot(soft, values * masks[h])
            mixed[here, lanes] = out.astype(BF)
            return carry

        lax.fori_loop(0, WHEADS // 2, attend, 0)

    value = word_in_out[...] + dot(mixed[...], weights[:, at_out : at_out + width])
    after[...] = value
    unit, spread = norm_parts(value)
    unit_two[...] = unit
    normed_two[...] = (unit * small_rows[2:3, :] + small_rows[3:4, :]).astype(BF)
    row = lax.broadcasted_iota(jnp.int32, (own_words, 1), 0)
    index = jnp.where(row < local, origin[0] + row, origin[1] + row - local)
    valid = index < length
    up_low[...] = jnp.where(valid, cotangent[...].astype(F32), 0.0).astype(BF)
    total[...] = jnp.zeros_like(total)
    grad_normed[...] = jnp.zeros_like(grad_normed)

    def feed(j, carry):
        expand = weights[:, pl.ds(pl.multiple_of(at_expand + j * width, GROUP), width)]
        shrink = weights[:, pl.ds(pl.multiple_of(at_reduce + j * width, GROUP), width)]
        pre = dot(normed_two[...], expand) + small_rows[pl.ds(6 + j, 1), :]
        act, slope = gelu_both(pre)
        act = act.astype(BF)
        total[...] += dot(act, shrink)
        grad_pre = dot_t(up_low[...], shrink) * slope
        sums_out[pl.ds(6 + j, 1), :] = jnp.sum(grad_pre, 0, keepdims=True)
        grad_pre = grad_pre.astype(BF)
        grad_normed[...] += dot_t(grad_pre, expand)
        cols = pl.multiple_of(j * width, GROUP)
        grads[:, pl.ds(cols, width)] = t_dot(normed_two[...], grad_pre).astype(BF)
        grads[:, pl.ds(pl.multiple_of(hidden + j * width, GROUP), width)] = t_dot(
            act, up_low[...]
        ).astype(BF)
        return carry

    lax.fori_loop(0, FOLD, feed, 0)
    words_out[...] = jnp.where(valid, after[...] + (total[...] + small_rows[4:5, :]), 0.0)
    upstream = up_low[...].astype(F32)
    incoming = grad_normed[...]
    sums_out[2:3, :] = jnp.sum(incoming * unit_two[...], 0, keepdims=True)
    sums_out[3:4, :] = jnp.sum(incoming, 0, keepdims=True)
    sums_out[4:5, :] = jnp.sum(upstream, 0, keepdims=True)
    grad_after = upstream + norm_back(unit_two[...], spread, incoming * small_rows[2:3, :])
    grad_after_out[...] = grad_after
    grad_low = grad_after.astype(BF)
    grads[:, 2 * hidden :] = t_dot(mixed[...], grad_low).astype(BF)
    mixed[...] = dot_t(grad_low, weights[:, at_out : at_out + width]).astype(BF)

    def attend_back(p, carry):
        lanes = pl.ds(pl.multiple_of(p * GROUP, GROUP), GROUP)
        after_lanes = pl.ds(pl.multiple_of(width + p * GROUP, GROUP), GROUP)
        grad_keys, grad_values = [], []
        for t in range(2):
            here = slice(t * local, (t + 1) * local)
            keys_seen = reach[t]
            asking = query[here, lanes]
            keys = pair[:keys_seen, lanes]
            values = pair[:keys_seen, after_lanes]
            incoming = mixed[here, lanes]
            grad_query = jnp.zeros((local, GROUP), F32)
            grad_key = jnp.zeros((keys_seen, GROUP), F32)
            grad_value = jnp.zeros((keys_seen, GROUP), F32)
            for h in range(2):
                soft = softs[t][2 * p + h]
                wide = soft.astype(F32)
                one = dot_t(incoming * masks[h], values)
                one = wide * (one - jnp.sum(wide * one, -1, keepdims=True))
                one = one.astype(BF)
                grad_query = grad_query + dot(one, keys * masks[h])
                grad_key = grad_key + t_dot(one, asking * masks[h])
                grad_value = grad_value + t_dot(soft, incoming * masks[h])
            grad_query_out[here, lanes] = (grad_query * SCALE).astype(BF)
            grad_keys.append(grad_key)
            grad_values.append(grad_value)
        for parts, at, factor in ((grad_keys, lanes, SCALE), (grad_values, after_lanes, 1.0)):
            grad_pair_out[:half, at] = ((parts[0] + parts[1][:half]) * factor).astype(BF)
            grad_pair_out[half:, at] = (parts[1][half:] * factor).astype(BF)
        return carry

    lax.fori_loop(0, WHEADS // 2, attend_back, 0)


def word_part(place, pooled, to_word, weights, cotangent):
    all_words, _ = pooled.shape
    width = to_word.shape[1]
    own = cotangent.shape[0]
    local = own // 2
    hidden = FOLD * width
    vmem = pl.BlockSpec(memory_space=pltpu.VMEM)
    return pl.pallas_call(
        word_kernel,
        out_shape=(
            jax.ShapeDtypeStruct((own, width), F32),
            jax.ShapeDtypeStruct((own, width), F32),
            jax.ShapeDtypeStruct((own, width), BF),
            jax.ShapeDtypeStruct((all_words, 2 * width), BF),
            jax.ShapeDtypeStruct((own, width), BF),
            jax.ShapeDtypeStruct((own, width), F32),
            jax.ShapeDtypeStruct((width, 2 * hidden + width), BF),
            jax.ShapeDtypeStruct((16, width), F32),
        ),
        in_specs=[pl.BlockSpec(memory_space=pltpu.SMEM), vmem, vmem, vmem, vmem],
        out_specs=(vmem,) * 8,
        scratch_shapes=[
            pltpu.VMEM((SMALL, width), F32),
            pltpu.VMEM((all_words, width), F32),
            pltpu.VMEM((all_words, width), BF),
            pltpu.VMEM((all_words, 2 * width), BF),
            pltpu.VMEM((own, width), BF),
            pltpu.VMEM((local, all_words), F32),
            pltpu.VMEM((WHEADS, local, all_words // 2), BF),
            pltpu.VMEM((WHEADS, local, all_words), BF),
            pltpu.VMEM((own, width), BF),
            pltpu.VMEM((own, width), F32),
            pltpu.VMEM((own, width), F32),
            pltpu.VMEM((own, width), BF),
            pltpu.VMEM((own, width), BF),
            pltpu.VMEM((own, width), F32),
            pltpu.VMEM((own, width), F32),
        ],
        compiler_params=pltpu.CompilerParams(vmem_limit_bytes=56 * MIB),
        cost_estimate=pl.CostEstimate(
            flops=own * width * width * 60, bytes_accessed=20 * MIB, transcendentals=own * 8192
        ),
    )(place, pooled, to_word, weights, cotangent)


def word_end_kernel(
    pooled,
    to_word,
    weights,
    small,
    grad_query,
    grad_pair,
    normed,
    word_in,
    grad_after,
    sums,
    grad_pooled,
    grad_to_word,
    grads,
    small_rows,
    small_grads,
    incoming,
):
    width = to_word.shape[1]
    small_rows[...] = small[...].astype(F32).T
    incoming[:, :width] = grad_query[...]
    incoming[:, width:] = grad_pair[...].astype(BF)
    grads[:, : 3 * width] = t_dot(normed[...], incoming[...]).astype(BF)
    grad_normed = dot_t(incoming[...], weights[...])
    unit, spread = norm_parts(word_in[...])
    small_grads[...] = jnp.zeros_like(small_grads)
    small_grads[0:1, :] = jnp.sum(grad_normed * unit, 0, keepdims=True)
    small_grads[1:2, :] = jnp.sum(grad_normed, 0, keepdims=True)
    small_grads[2:5, :] = sums[2:5, :]
    small_grads[6:10, :] = sums[6:10, :]
    value = grad_after[...] + norm_back(unit, spread, grad_normed * small_rows[0:1, :])
    small_grads[5:6, :] = jnp.sum(value, 0, keepdims=True)
    low = value.astype(BF)
    grad_to_word[...] = t_dot(pooled[...], low).astype(BF)
    grad_pooled[...] = dot_t(low, to_word[...]).astype(BF)
    grads[:, 3 * width :] = small_grads[...].T.astype(BF)


def word_end(pooled, to_word, weights, grad_query, grad_pair, normed, word_in, grad_after, sums):
    own, narrow = pooled.shape
    width = to_word.shape[1]
    columns = weights.shape[1]
    return pl.pallas_call(
        word_end_kernel,
        grid=(1,),
        out_shape=(
            jax.ShapeDtypeStruct((own, narrow), BF),
            jax.ShapeDtypeStruct((narrow, width), BF),
            jax.ShapeDtypeStruct((width, 3 * width + SMALL), BF),
        ),
        in_specs=[
            full(pooled.shape),
            full(to_word.shape),
            pl.BlockSpec((width, 3 * width), lambda i: (0, 0)),
            pl.BlockSpec((width, SMALL), lambda i: (0, columns // SMALL - 1)),
            full(grad_query.shape),
            full(grad_pair.shape),
            full(normed.shape),
            full(word_in.shape),
            full(grad_after.shape),
            full(sums.shape),
        ],
        out_specs=(full((own, narrow)), full((narrow, width)), full((width, 3 * width + SMALL))),
        scratch_shapes=[
            pltpu.VMEM((SMALL, width), F32),
            pltpu.VMEM((SMALL, width), F32),
            pltpu.VMEM((own, 3 * width), BF),
        ],
        compiler_params=pltpu.CompilerParams(vmem_limit_bytes=48 * MIB),
        cost_estimate=pl.CostEstimate(
            flops=own * width * width * 14, bytes_accessed=10 * MIB, transcendentals=0
        ),
    )(pooled, to_word, weights, weights, grad_query, grad_pair, normed, word_in, grad_after, sums)


def swap(values, axis, bit):
    count = lax.axis_size(axis)
    return lax.ppermute(values, axis, [(k, k ^ bit) for k in range(count)])


def bit_of(axis, bit):
    return lax.rem(lax.div(lax.axis_index(axis), bit), 2)


def bits_down(axis):
    count = lax.axis_size(axis)
    return [1 << k for k in reversed(range(count.bit_length() - 1))]


def ordered(mine, other, axis, bit, at):
    swapped = bit_of(axis, bit) == 1
    low = jnp.where(swapped, other, mine)
    high = jnp.where(swapped, mine, other)
    return jnp.stack([low, high], at)


def gather(shard):
    value = shard
    for axis in ("dp", "fsdp"):
        for bit in bits_down(axis):
            value = ordered(value, swap(value, axis, bit), axis, bit, value.ndim - 2)
    return value.reshape(-1, shard.shape[-1])


def scatter(value):
    steps = [(axis, bit) for axis in ("dp", "fsdp") for bit in bits_down(axis)]
    rows, columns = value.shape
    value = value.reshape([2] * len(steps) + [rows >> len(steps), columns])
    for axis, bit in reversed(steps):
        mine = bit_of(axis, bit)
        at = value.ndim - 3
        kept = lax.dynamic_index_in_dim(value, mine, at, keepdims=False)
        sent = lax.dynamic_index_in_dim(value, 1 - mine, at, keepdims=False)
        value = kept.astype(F32) + swap(sent, axis, bit).astype(F32)
        if value.ndim > 2:
            value = value.astype(BF)
    return value


def split_hidden(shard):
    rows, hidden = shard.shape
    return shard.reshape(rows, hidden // FOLD, FOLD).swapaxes(1, 2).reshape(rows, hidden)


def join_hidden(shard):
    rows, hidden = shard.shape
    return shard.reshape(rows, FOLD, hidden // FOLD).swapaxes(1, 2).reshape(rows, hidden)


def beside(columns):
    rows = columns[0].shape[0]
    small = jnp.concatenate(columns, 1)
    return jnp.pad(small, ((0, 0), (0, SMALL - small.shape[1])))


def body(
    char_inputs,
    language_ids,
    char_counts,
    row_lengths,
    cotangent,
    language_table,
    char_gain_one,
    char_bias_one,
    char_inward,
    char_outward,
    char_gain_two,
    char_bias_two,
    char_expand,
    char_expand_bias,
    char_reduce,
    char_reduce_bias,
    char_to_word,
    char_to_word_bias,
    word_gain_one,
    word_bias_one,
    word_inward,
    word_outward,
    word_gain_two,
    word_bias_two,
    word_expand,
    word_expand_bias,
    word_reduce,
    word_reduce_bias,
):
    rows, local, slots, width = char_inputs.shape
    words = rows * local
    langs = language_table.shape[0]
    wide = word_inward.shape[1] // 3
    share = lax.axis_size("fsdp")
    members = share // rows
    member = lax.rem(lax.axis_index("fsdp"), members)
    top = members
    my_row = bit_of("fsdp", top)

    def one(vector, like):
        return vector.reshape(like.shape[0], -1)

    attend_shard = jnp.concatenate(
        [
            char_inward,
            char_outward,
            beside(
                [language_table.T]
                + [
                    one(v, char_inward)
                    for v in (
                        char_gain_one,
                        char_bias_one,
                        char_gain_two,
                        char_bias_two,
                        char_reduce_bias,
                        char_expand_bias,
                    )
                ]
            ),
        ],
        1,
    )
    feed_shard = jnp.concatenate(
        [split_hidden(char_expand), one(char_reduce, char_inward), char_to_word], 1
    )
    word_shard = jnp.concatenate(
        [
            word_inward,
            word_outward,
            split_hidden(word_expand),
            one(word_reduce, word_inward),
            beside(
                [
                    one(v, word_inward)
                    for v in (
                        word_gain_one,
                        word_bias_one,
                        word_gain_two,
                        word_bias_two,
                        word_reduce_bias,
                        char_to_word_bias,
                        word_expand_bias,
                    )
                ]
            ),
        ],
        1,
    )
    attend_full = gather(attend_shard)
    feed_full = gather(feed_shard)
    word_full = lax.all_gather(word_shard, ("dp", "fsdp"), axis=0, tiled=True)
    to_word = feed_full[:, 2 * FOLD * width :]

    def pick(values, which):
        return lax.dynamic_index_in_dim(values, which, 0, keepdims=False)

    def to_rows(values):
        other = swap(pick(values, 1 - my_row), "fsdp", top)
        return ordered(pick(values, my_row), other, "fsdp", top, 0)

    cotangent_own = to_rows(cotangent)
    counts = char_counts.reshape(words)
    inverse = 1.0 / counts.astype(F32).reshape(words, 1)
    packed, bias, hot, offs, first, rows_of, blocks = pack(
        counts, char_inputs.reshape(words, slots, width), local
    )
    qkv, soft, mixed, after = char_attend(langs, blocks, rows_of, language_ids, packed, bias, attend_full)
    act, slope, pooled = char_ffn(langs, blocks, first, after, hot, inverse, attend_full, feed_full)

    pooled_own = to_rows(pooled.reshape(rows, local, width))
    pooled_all = pooled_own[:, None]
    for bit in [b for b in bits_down("fsdp") if b < members]:
        both = ordered(pooled_all, swap(pooled_all, "fsdp", bit), "fsdp", bit, 2)
        pooled_all = both.reshape(rows, -1, local, width)
    place = jnp.stack([member, pick(row_lengths, my_row)])
    (
        words_own,
        word_after_grad,
        query_grad,
        pair_grad,
        word_normed,
        word_in,
        word_grads,
        word_sums,
    ) = word_part(
        place,
        pooled_all.reshape(-1, width),
        to_word,
        word_full,
        cotangent_own.reshape(words, wide),
    )
    word_shares = scatter(word_grads)
    words_out = to_rows(words_own.reshape(rows, local, wide))
    pair_own = pair_grad.reshape(rows, members, local, 2 * wide)
    for bit in [b for b in bits_down("fsdp") if b < members]:
        halves = pair_own.reshape(rows, 2, -1, local, 2 * wide)
        mine = bit_of("fsdp", bit)
        kept = lax.dynamic_index_in_dim(halves, mine, 1, keepdims=False)
        sent = lax.dynamic_index_in_dim(halves, 1 - mine, 1, keepdims=False)
        pair_own = (kept.astype(F32) + swap(sent, "fsdp", bit).astype(F32)).astype(BF)
    pooled_grad, to_word_grad, inward_grads = word_end(
        pooled_own.reshape(words, width),
        to_word,
        word_full,
        query_grad,
        pair_own.reshape(words, 2 * wide),
        word_normed,
        word_in,
        word_after_grad,
        word_sums,
    )
    inward_shares = scatter(inward_grads)
    char_up = to_rows(pooled_grad.reshape(rows, local, width)).reshape(words, width)
    after_grad, feed_grads, char_sums = char_ffn_back(
        langs,
        blocks,
        first,
        after,
        hot,
        act,
        slope,
        inverse,
        char_up,
        attend_full,
        feed_full,
        to_word_grad,
    )
    feed_shares = scatter(feed_grads)
    attend_grads, *start_grad = char_attend_back(
        langs, blocks, rows_of, language_ids, packed, qkv, soft, mixed, after_grad, attend_full, char_sums
    )
    attend_shares = scatter(attend_grads)
    char_input_grad = unpack(offs, counts, start_grad, words, slots).reshape(char_inputs.shape)

    small = attend_shares[:, 4 * width :]
    word_small = inward_shares[:, 3 * wide :]
    hidden = FOLD * width
    wide_hidden = FOLD * wide

    def column(values, at, count=1):
        return values[:, at : at + count].reshape(-1)

    return (
        words_out,
        char_input_grad,
        small[:, :langs].T,
        column(small, langs),
        column(small, langs + 1),
        attend_shares[:, : 3 * width],
        attend_shares[:, 3 * width : 4 * width],
        column(small, langs + 2),
        column(small, langs + 3),
        join_hidden(feed_shares[:, :hidden]),
        column(small, langs + 5, FOLD),
        feed_shares[:, hidden : 2 * hidden].reshape(char_reduce.shape),
        column(small, langs + 4),
        feed_shares[:, 2 * hidden :],
        column(word_small, 5),
        column(word_small, 0),
        column(word_small, 1),
        inward_shares[:, : 3 * wide],
        word_shares[:, 2 * wide_hidden :],
        column(word_small, 2),
        column(word_small, 3),
        join_hidden(word_shares[:, :wide_hidden]),
        column(word_small, 6, FOLD),
        word_shares[:, wide_hidden : 2 * wide_hidden].reshape(word_reduce.shape),
        column(word_small, 4),
    )


def solution(mesh):
    both = ("dp", "fsdp")
    vector, matrix = P(both), P(both, None)
    weights = (
        (P(None, both), vector, vector, matrix, matrix, vector, vector)
        + (matrix, vector, matrix, vector, matrix, vector)
        + (vector, vector, matrix, matrix, vector, vector, matrix, vector, matrix, vector)
    )
    in_specs = (
        P("dp", "fsdp", None, None),
        P("dp"),
        P("dp", "fsdp"),
        P("dp"),
        P("dp", "fsdp", None),
    ) + weights
    out_specs = (P("dp", "fsdp", None), P("dp", "fsdp", None, None)) + weights
    return jax.shard_map(body, mesh=mesh, in_specs=in_specs, out_specs=out_specs, check_vma=False)
```

time: 1920 us -> 403 us (0.21)
  waiting for transfers between devices: 847 us -> 96.4 us
  blocking collectives: 361 us -> 0 us
  matrix products: 306 us -> 0 us
  local copies, waits for them, and re-layouts: 302 us -> 41.1 us
  Pallas kernels: 0 us -> 190 us
  other arithmetic: 69.8 us -> 15.6 us
  starting transfers between devices: 1.36 us -> 44.7 us
    reduce_scatter x10 -> x0, waiting for transfers between devices: 773 us -> none  [the longest x1 137 us: body(): lax.psum_scatter(char_grads[9], ('dp', 'fsdp'), scatter_dimension=0, tile...]
    dot_general x41 -> x0, matrix products: 306 us -> none  [the longest x9 74.7 us: back_product(): lax.dot_general(grad_low, weight, (((grad_low.ndim - 1,), (1,)), ((), ())...]
    all_gather x7 -> x0, blocking collectives: 275 us -> none  [the longest x1 42.6 us: body(): lax.all_gather(word_outward, ('dp', 'fsdp'), axis=0, tiled=True)]
    pallas_call x0 -> x8, Pallas kernels: none -> 190 us  [the longest x1 40.6 us: word_part(): pl.pallas_call(word_kernel, out_shape=(jax.ShapeDtypeStruct((own, width),...]
    reshape x14 -> x22, local copies, waits for them, and re-layouts: 127 us -> 13.8 us  [the longest x15 10.6 us: one(): return vector.reshape(like.shape[0], -1)]
    ppermute x0 -> x36, waiting for transfers between devices: none -> 96.4 us  [swap(): return lax.ppermute(values, axis, [(k, k ^ bit) for k in range(count)])]
    unnamed x2 -> x0, blocking collectives: 86.1 us -> none
    all_gather x4 -> x1, waiting for transfers between devices: 71.4 us -> 0.01 us  [body(): word_full = lax.all_gather(word_shard, ('dp', 'fsdp'), axis=0, tiled=True)]
  transfers between devices with their start and end apart: 14 -> 37, of which waited for: 9 -> 20; matrix products, arithmetic and copies ran while one was open for 32% -> 9% of each run, Pallas kernels for 0% -> 36%
where the time goes in v1:
time: 403 us
  Pallas kernels  190 us (47%)
  waiting for transfers between devices  96.4 us (24%)
  starting transfers between devices  44.7 us (11%)
  local copies, waits for them, and re-layouts  41.1 us (10%)
  other arithmetic  15.6 us (4%)
  between operations  15.1 us (4%)
    ppermute x36, waiting for transfers between devices, swap(): return lax.ppermute(values, axis, [(k, k ^ bit) for k in range(count)])  96.4 us
    ppermute x36, starting transfers between devices, swap(): return lax.ppermute(values, axis, [(k, k ^ bit) for k in range(count)])  44.6 us
    pallas_call x1, Pallas kernels, word_part(): pl.pallas_call(word_kernel, out_shape=(jax.ShapeDtypeStruct((own, width),...  40.6 us
    pallas_call x1, Pallas kernels, char_attend_back(): pl.pallas_call(functools.partial(char_attend_back_kernel, langs), out_sha...  39.7 us
    pallas_call x1, Pallas kernels, char_attend(): pl.pallas_call(functools.partial(char_attend_kernel, langs), out_shape=(j...  26.8 us
    pallas_call x1, Pallas kernels, char_ffn_back(): pl.pallas_call(functools.partial(char_ffn_back_kernel, langs), out_shape=...  24.9 us
    pallas_call x1, Pallas kernels, char_ffn(): pl.pallas_call(functools.partial(char_ffn_kernel, langs), out_shape=(jax....  22.7 us
    pallas_call x1, Pallas kernels, pack(): pl.pallas_call(functools.partial(pack_kernel, per_row), out_shape=(jax.Sh...  20.4 us
  transfers between devices with their start and end apart: 37, of which 20 were waited for; matrix products, arithmetic and copies ran while one was open for 9% of the time, Pallas kernels for 36%

profile of v1, /device:TPU:0, one launch (start us, length us, event | category | flops | bytes accessed | tf_op | source)
XLA Modules:
  0.0 402.6 jit_solution(9273692006266540294)
XLA Ops:
  23.2 4.0 %collective-permute-start = (bf16[8,1152]{1,0:T(8,128)(2,1)S(1)}, bf16[8,1152]{1,0:T(8,128)(2,1)S(1)}, u32[]{:S(2)}, u32[]{:S(2)}) collective-permute-start(bf16[8,1152]{1,0:T(8,128)(2,1)S(1)} %fusion.26), channel_id=1, source_target_pairs={{0,16},{4,20},{8,24},{12,28},{16,0},{20,4},{24,8},{28,12},{1,17},{... | collective-permute-start | bytes 55304 | tf_op jit(solution)/shard_map/ppermute | solution.py:889
  28.7 20.4 %shard_map.459 = (bf16[9728,256]{1,0:T(8,128)(2,1)}, bf16[9728,128]{1,0:T(8,128)(2,1)S(1)}, bf16[9728,128]{1,0:T(8,128)(2,1)S(1)}, s32[512]{0:T(512)S(1)}, s32[7...) custom-call(s32[512]{0:T(512)S(1)} %bitcast.297, bf16[512,16,256]{2,1,0:T(8,128)(2,1)} %bitcast.304), custom_call_target="tpu_custom_call" | custom-call | flops 9961472 | bytes 14942208 | tf_op jit(solution)/shard_map/pallas_call | solution.py:142
  51.3 2.8 collective-permute-done.1
  54.2 3.0 collective-permute-start.2
  67.4 15.2 %collective-permute-done.8 = bf16[2,2,2,8,2560]{4,3,0,1,2:T(8,128)(2,1)S(1)} collective-permute-done((bf16[2,2,2,8,2560]{4,3,0,1,2:T(8,128)(2,1)S(1)}, bf16[2,2,2,8,2560]{4,3,0,1,2:T(8,128)(2,1)S(1)}, u32[]{:S(2)}, u32[]{:S(2)}) %collective-permute-start.8) | collective-permute-done | bytes 327712 | tf_op jit(solution)/shard_map/ppermute | solution.py:889
  82.8 26.8 %shard_map.460 = (bf16[9728,768]{1,0:T(8,128)(2,1)}, bf16[9728,512]{1,0:T(8,128)(2,1)}, bf16[9728,256]{1,0:T(8,128)(2,1)}, f32[9728,256]{1,0:T(8,128)}) custom-call(s32[1]{0:T(128)} %get-tuple-element.56.blocks, s32[76]{0:T(128)S(1)} %get-tuple-element.58.refs_0_, s32[2]{0:T(128)S(1)} %copy-done.12, bf16[9728,256]{1,0:T(8,128)(2,1)} %get-tuple-element.59.refs_2_, ...), custom_call_target="tpu_custom_call" | custom-call | flops 7650410496 | bytes 29884416 | tf_op jit(solution)/shard_map/pallas_call | solution.py:294
  110.0 22.7 %shard_map.461 = (bf16[9728,1024]{1,0:T(8,128)(2,1)}, bf16[9728,1024]{1,0:T(8,128)(2,1)}, bf16[512,256]{1,0:T(8,128)(2,1)S(1)}) custom-call(s32[1]{0:T(128)} %get-tuple-element.56.blocks, s32[76]{0:T(128)S(1)} %get-tuple-element.57.refs_0_, f32[9728,256]{1,0:T(8,128)} %get-tuple-element.61.refs_1_, bf16[9728,128]{1,0:T(8,128)(2,1)S(1)} %get-tuple-element.62.refs_2_, ...), custom_call_target="tpu_custom_call" | custom-call | flops 10200547328 | bytes 49807360 | tf_op jit(solution)/shard_map/pallas_call | solution.py:325
  143.1 40.6 %shard_map.462 = (f32[512,512]{1,0:T(8,128)}, f32[512,512]{1,0:T(8,128)}, bf16[512,512]{1,0:T(8,128)(2,1)}, bf16[1024,1024]{1,0:T(8,128)(2,1)}, bf16[512,512]{1,...) custom-call(s32[2]{0:T(128)} %pad_add_fusion.place, ...), custom_call_target="tpu_custom_call" | custom-call | flops 8053063680 | bytes 20971520 | tf_op jit(solution)/shard_map/pallas_call | solution.py:774
  186.1 3.0 collective-permute-done.14
  191.1 5.5 %shard_map.463 = (bf16[512,256]{1,0:T(8,128)(2,1)S(1)}, bf16[256,512]{1,0:T(8,128)(2,1)S(1)}, bf16[512,1664]{1,0:T(8,128)(2,1)}) custom-call(bf16[512,256]{1,0:T(8,128)(2,1)S(1)} %bitcast.284, bf16[256,512]{1,0:T(8,128)(2,1)S(1)} %copy-done, bf16[512,6272]{1,0:T(8,128)(2,1)} %all-gather.2.cloned.1.call-done.weights.small, ...), custom_call_target="tpu_custom_call" | custom-call | flops 1879048192 | bytes 10485760 | tf_op jit(solution)/shard_map/pallas_call | solution.py:854
  200.6 2.9 collective-permute-done.15
  205.4 24.9 %shard_map.464 = (f32[9728,256]{1,0:T(8,128)}, bf16[256,2560]{1,0:T(8,128)(2,1)S(1)}, f32[64,256]{1,0:T(8,128)S(1)}) custom-call(s32[1]{0:T(128)} %get-tuple-element.56.blocks, s32[76]{0:T(128)S(1)} %get-tuple-element.57.refs_0_, f32[9728,256]{1,0:T(8,128)} %get-tuple-element.61.refs_1_, bf16[9728,128]{1,0:T(8,128)(2,1)} %copy-done.9, ...), custom_call_target="tpu_custom_call" | custom-call | flops 20401094656 | bytes 49807360 | tf_op jit(solution)/shard_map/pallas_call | solution.py:435
  230.3 39.7 %shard_map.465 = (bf16[256,1152]{1,0:T(8,128)(2,1)S(1)}, f32[9856,128]{1,0:T(8,128)}, f32[9856,128]{1,0:T(8,128)}) custom-call(s32[1]{0:T(128)} %get-tuple-element.56.blocks, s32[76]{0:T(128)S(1)} %get-tuple-element.58.refs_0_, s32[2]{0:T(128)S(1)} %copy-done.12, bf16[9728,256]{1,0:T(8,128)(2,1)} %get-tuple-element.59.refs_2_, ...), custom_call_target="tpu_custom_call" | custom-call | flops 15300820992 | bytes 49807360 | tf_op jit(solution)/shard_map/pallas_call | solution.py:565
  273.0 5.6 %collective-permute-done.17 = bf16[2,2,2,8,1152]{4,3,0,1,2:T(8,128)(2,1)S(1)} collective-permute-done((bf16[2,2,2,8,1152]{4,3,0,1,2:T(8,128)(2,1)S(1)}, bf16[2,2,2,8,1152]{4,3,0,1,2:T(8,128)(2,1)S(1)}, u32[]{:S(2)}, u32[]{:S(2)}) %collective-permute-start.17) | collective-permute-done | bytes 147488 | tf_op jit(solution)/shard_map/ppermute | solution.py:889
  278.7 6.6 %collective-permute-start.18 = (bf16[2,2,8,1152]{3,2,0,1:T(8,128)(2,1)S(1)}, bf16[2,2,8,1152]{3,2,0,1:T(8,128)(2,1)S(1)}, u32[]{:S(2)}, u32[]{:S(2)}) collective-permute-start(bf16[2,2,8,1152]{3,2,0,1:T(8,128)(2,1)S(1)} %dynamic-slice_bitcast_fusion.16), channel_id=1, source_target_pairs={{0,4},{4,0},{8,12},{12,8},{16,20},{20,16},{24,28},{28,24},{1,5},{5... | collective-permute-start | bytes 221192 | tf_op jit(solution)/shard_map/ppermute | solution.py:889
  288.9 2.8 collective-permute-done.19
  294.5 9.2 %shard_map.466 = f32[512,16,256]{2,1,0:T(8,128)} custom-call(s32[512]{0:T(512)S(1)} %get-tuple-element.65.offs, s32[512]{0:T(512)S(1)} %bitcast.298, f32[9856,128]{1,0:T(8,128)S(1)} %bitcast.278, f32[9856,128]{1,0:T(8,128)} %get-tuple-element.82.refs_1_), custom_call_target="tpu_custom_call" | custom-call | flops 2097152 | bytes 16777216 | tf_op jit(solution)/shard_map/pallas_call | solution.py:182
  311.7 7.0 %collective-permute-done.22 = bf16[2,2,2,8,2560]{4,3,0,1,2:T(8,128)(2,1)S(1)} collective-permute-done((bf16[2,2,2,8,2560]{4,3,0,1,2:T(8,128)(2,1)S(1)}, bf16[2,2,2,8,2560]{4,3,0,1,2:T(8,128)(2,1)S(1)}, u32[]{:S(2)}, u32[]{:S(2)}) %collective-permute-start.22) | collective-permute-done | bytes 327712 | tf_op jit(solution)/shard_map/ppermute | solution.py:889
  320.7 4.0 collective-permute-done.23
  326.8 4.5 %collective-permute-done.27 = bf16[2,2,2,16,1664]{4,3,0,1,2:T(8,128)(2,1)S(1)} collective-permute-done((bf16[2,2,2,16,1664]{4,3,0,1,2:T(8,128)(2,1)S(1)}, bf16[2,2,2,16,1664]{4,3,0,1,2:T(8,128)(2,1)S(1)}, u32[]{:S(2)}, u32[]{:S(2)}) %collective-permute-start.27) | collective-permute-done | bytes 426016 | tf_op jit(solution)/shard_map/ppermute | solution.py:889
  343.4 18.4 %collective-permute-done.32 = bf16[2,2,2,16,4608]{4,3,0,1,2:T(8,128)(2,1)} collective-permute-done((bf16[2,2,2,16,4608]{4,3,0,1,2:T(8,128)(2,1)S(1)}, bf16[2,2,2,16,4608]{4,3,0,1,2:T(8,128)(2,1)}, u32[]{:S(2)}, u32[]{:S(2)}) %collective-permute-start.32) | collective-permute-done | bytes 1179680 | tf_op jit(solution)/shard_map/ppermute | solution.py:889
  366.8 9.9 %collective-permute-done.33 = bf16[2,2,16,4608]{3,2,0,1:T(8,128)(2,1)S(1)} collective-permute-done((bf16[2,2,16,4608]{3,2,0,1:T(8,128)(2,1)S(1)}, bf16[2,2,16,4608]{3,2,0,1:T(8,128)(2,1)S(1)}, u32[]{:S(2)}, u32[]{:S(2)}) %collective-permute-start.33) | collective-permute-done | bytes 589856 | tf_op jit(solution)/shard_map/ppermute | solution.py:889
  379.9 5.2 %collective-permute-done.34 = bf16[2,16,4608]{2,1,0:T(8,128)(2,1)S(1)} collective-permute-done((bf16[2,16,4608]{2,1,0:T(8,128)(2,1)S(1)}, bf16[2,16,4608]{2,1,0:T(8,128)(2,1)S(1)}, u32[]{:S(2)}, u32[]{:S(2)}) %collective-permute-start.34) | collective-permute-done | bytes 294944 | tf_op jit(solution)/shard_map/ppermute | solution.py:889
  385.2 3.1 collective-permute-start.35
  (259 shorter events, 99.8 us)
Async XLA Ops:
  7.2 135.9 %all-gather.2.cloned.1.call-start = ((), (), s32[]{:S(2)}) async-start(), calls=%async_computation | async-start | bytes 6623232 | tf_op jit(solution)/shard_map/all_gather | solution.py:1039
  23.2 25.9 %collective-permute-start = (bf16[8,1152]{1,0:T(8,128)(2,1)S(1)}, bf16[8,1152]{1,0:T(8,128)(2,1)S(1)}, u32[]{:S(2)}, u32[]{:S(2)}) collective-permute-start(bf16[8,1152]{1,0:T(8,128)(2,1)S(1)} %fusion.26), channel_id=1, source_target_pairs={{0,16},{4,20},{8,24},{12,28},{16,0},{20,4},{24,8},{28,12},{1,17},{... | collective-permute-start | bytes 55304 | tf_op jit(solution)/shard_map/ppermute | solution.py:889
  28.3 22.3 %collective-permute-start.5 = (bf16[8,2560]{1,0:T(8,128)(2,1)S(1)}, bf16[8,2560]{1,0:T(8,128)(2,1)S(1)}, u32[]{:S(2)}, u32[]{:S(2)}) collective-permute-start(bf16[8,2560]{1,0:T(8,128)(2,1)S(1)} %constant_dynamic-update-slice_fusion), channel_id=1, source_target_pairs={{0,16},{4,20},{8,24},{12,28},{16,0},{20,4},{24,8},{28,12},{1,17},{... | collective-permute-start | bytes 122888 | tf_op jit(solution)/shard_map/ppermute | solution.py:889
  50.7 6.5 %collective-permute-start.6 = (bf16[2,8,2560]{2,1,0:T(8,128)(2,1)S(1)}, bf16[2,8,2560]{2,1,0:T(8,128)(2,1)S(1)}, u32[]{:S(2)}, u32[]{:S(2)}) collective-permute-start(bf16[2,8,2560]{2,1,0:T(8,128)(2,1)S(1)} %pad_maximum_fusion.12), channel_id=1, source_target_pairs={{0,8},{4,12},{8,0},{12,4},{16,24},{20,28},{24,16},{28,20},{1,9},{5... | collective-permute-start | bytes 245768 | tf_op jit(solution)/shard_map/ppermute | solution.py:889
  66.6 16.0 %collective-permute-start.8 = (bf16[2,2,2,8,2560]{4,3,0,1,2:T(8,128)(2,1)S(1)}, bf16[2,2,2,8,2560]{4,3,0,1,2:T(8,128)(2,1)S(1)}, u32[]{:S(2)}, u32[]{:S(2)}) collective-permute-start(bf16[2,2,2,8,2560]{4,3,0,1,2:T(8,128)(2,1)S(1)} %pad_maximum_fusion.6), channel_id=1, source_target_pairs={{0,2},{1,3},{2,0},{3,1},{4,6},{5,7},{6,4},{7,5},{8,10},{9,11},{10,... | collective-permute-start | bytes 983048 | tf_op jit(solution)/shard_map/ppermute | solution.py:889
  82.7 26.9 %collective-permute-start.9 = (bf16[2,2,2,2,8,2560]{5,4,0,1,2,3:T(8,128)(2,1)S(1)}, bf16[2,2,2,2,8,2560]{5,4,0,1,2,3:T(8,128)(2,1)S(1)}, u32[]{:S(2)}, u32[]{:S(2)}) collective-permute-start(bf16[2,2,2,2,8,2560]{5,4,0,1,2,3:T(8,128)(2,1)S(1)} %pad_maximum_fusion.2), channel_id=1, source_target_pairs={{0,1},{1,0},{2,3},{3,2},{4,5},{5,4},{6,7},{7,6},{8,9},{9,8},{10,11... | collective-permute-start | bytes 1966088 | tf_op jit(solution)/shard_map/ppermute | solution.py:889
  132.8 7.7 %collective-permute-start.12 = (bf16[256,512]{1,0:T(8,128)(2,1)S(1)}, bf16[256,512]{1,0:T(8,128)(2,1)S(1)}, u32[]{:S(2)}, u32[]{:S(2)}) collective-permute-start(bf16[256,512]{1,0:T(8,128)(2,1)S(1)} %dynamic-slice_bitcast_fusion.7), channel_id=1, source_target_pairs={{0,2},{1,3},{2,0},{3,1},{4,6},{5,7},{6,4},{7,5},{8,10},{9,11},{10,... | collective-permute-start | bytes 786440 | tf_op jit(solution)/shard_map/ppermute | solution.py:889
  197.4 6.1 %collective-permute-start.15 = (bf16[256,256]{1,0:T(8,128)(2,1)S(1)}, bf16[256,256]{1,0:T(8,128)(2,1)S(1)}, u32[]{:S(2)}, u32[]{:S(2)}) collective-permute-start(bf16[256,256]{1,0:T(8,128)(2,1)S(1)} %dynamic-slice_bitcast_fusion.12), channel_id=1, source_target_pairs={{0,2},{1,3},{2,0},{3,1},{4,6},{5,7},{6,4},{7,5},{8,10},{9,11},{10,... | collective-permute-start | bytes 393224 | tf_op jit(solution)/shard_map/ppermute | solution.py:889
  199.9 72.9 %collective-permute-start.13 = (f32[256,512]{1,0:T(8,128)S(1)}, f32[256,512]{1,0:T(8,128)S(1)}, u32[]{:S(2)}, u32[]{:S(2)}) collective-permute-start(f32[256,512]{1,0:T(8,128)S(1)} %dynamic-slice_bitcast_fusion.3), channel_id=1, source_target_pairs={{0,2},{1,3},{2,0},{3,1},{4,6},{5,7},{6,4},{7,5},{8,10},{9,11},{10,... | collective-permute-start | bytes 1572872 | tf_op jit(solution)/shard_map/ppermute | solution.py:889
  272.1 59.3 %collective-permute-start.31 = (bf16[2,2,2,2,16,4608]{5,4,0,1,2,3:T(8,128)(2,1)}, bf16[2,2,2,2,16,4608]{5,4,0,1,2,3:T(8,128)(2,1)}, u32[]{:S(2)}, u32[]{:S(2)}) collective-permute-start(bf16[2,2,2,2,16,4608]{5,4,0,1,2,3:T(8,128)(2,1)} %bitcast.273), channel_id=1, source_target_pairs={{0,1},{1,0},{2,3},{3,2},{4,5},{5,4},{6,7},{7,6},{8,9},{9,8},{10,11... | collective-permute-start | bytes 7077896 | tf_op jit(solution)/shard_map/ppermute | solution.py:889
  278.7 9.0 %collective-permute-start.18 = (bf16[2,2,8,1152]{3,2,0,1:T(8,128)(2,1)S(1)}, bf16[2,2,8,1152]{3,2,0,1:T(8,128)(2,1)S(1)}, u32[]{:S(2)}, u32[]{:S(2)}) collective-permute-start(bf16[2,2,8,1152]{3,2,0,1:T(8,128)(2,1)S(1)} %dynamic-slice_bitcast_fusion.16), channel_id=1, source_target_pairs={{0,4},{4,0},{8,12},{12,8},{16,20},{20,16},{24,28},{28,24},{1,5},{5... | collective-permute-start | bytes 221192 | tf_op jit(solution)/shard_map/ppermute | solution.py:889
  288.9 21.4 %collective-permute-start.26 = (bf16[2,2,2,2,16,1664]{5,4,0,1,2,3:T(8,128)(2,1)}, bf16[2,2,2,2,16,1664]{5,4,0,1,2,3:T(8,128)(2,1)}, u32[]{:S(2)}, u32[]{:S(2)}) collective-permute-start(bf16[2,2,2,2,16,1664]{5,4,0,1,2,3:T(8,128)(2,1)} %bitcast.274), channel_id=1, source_target_pairs={{0,1},{1,0},{2,3},{3,2},{4,5},{5,4},{6,7},{7,6},{8,9},{9,8},{10,11... | collective-permute-start | bytes 2555912 | tf_op jit(solution)/shard_map/ppermute | solution.py:889
  291.7 12.0 %collective-permute-start.20 = (bf16[8,1152]{1,0:T(8,128)(2,1)S(1)}, bf16[8,1152]{1,0:T(8,128)(2,1)S(1)}, u32[]{:S(2)}, u32[]{:S(2)}) collective-permute-start(bf16[8,1152]{1,0:T(8,128)(2,1)S(1)} %dynamic-slice_bitcast_fusion.20), channel_id=1, source_target_pairs={{0,16},{4,20},{8,24},{12,28},{16,0},{20,4},{24,8},{28,12},{1,17},{... | collective-permute-start | bytes 55304 | tf_op jit(solution)/shard_map/ppermute | solution.py:889
  294.5 12.5 %collective-permute-start.21 = (bf16[2,2,2,2,8,2560]{5,4,0,1,2,3:T(8,128)(2,1)}, bf16[2,2,2,2,8,2560]{5,4,0,1,2,3:T(8,128)(2,1)}, u32[]{:S(2)}, u32[]{:S(2)}) collective-permute-start(bf16[2,2,2,2,8,2560]{5,4,0,1,2,3:T(8,128)(2,1)} %bitcast.275), channel_id=1, source_target_pairs={{0,1},{1,0},{2,3},{3,2},{4,5},{5,4},{6,7},{7,6},{8,9},{9,8},{10,11... | collective-permute-start | bytes 1966088 | tf_op jit(solution)/shard_map/ppermute | solution.py:889
  308.5 10.2 %collective-permute-start.22 = (bf16[2,2,2,8,2560]{4,3,0,1,2:T(8,128)(2,1)S(1)}, bf16[2,2,2,8,2560]{4,3,0,1,2:T(8,128)(2,1)S(1)}, u32[]{:S(2)}, u32[]{:S(2)}) collective-permute-start(bf16[2,2,2,8,2560]{4,3,0,1,2:T(8,128)(2,1)S(1)} %dynamic-slice_bitcast_fusion.5), channel_id=1, source_target_pairs={{0,2},{1,3},{2,0},{3,1},{4,6},{5,7},{6,4},{7,5},{8,10},{9,11},{10,... | collective-permute-start | bytes 983048 | tf_op jit(solution)/shard_map/ppermute | solution.py:889
  320.1 11.2 %collective-permute-start.27 = (bf16[2,2,2,16,1664]{4,3,0,1,2:T(8,128)(2,1)S(1)}, bf16[2,2,2,16,1664]{4,3,0,1,2:T(8,128)(2,1)S(1)}, u32[]{:S(2)}, u32[]{:S(2)}) collective-permute-start(bf16[2,2,2,16,1664]{4,3,0,1,2:T(8,128)(2,1)S(1)} %dynamic-slice_bitcast_fusion.4), channel_id=1, source_target_pairs={{0,2},{1,3},{2,0},{3,1},{4,6},{5,7},{6,4},{7,5},{8,10},{9,11},{10,... | collective-permute-start | bytes 1277960 | tf_op jit(solution)/shard_map/ppermute | solution.py:889
  324.7 11.4 %collective-permute-start.24 = (bf16[2,8,2560]{2,1,0:T(8,128)(2,1)S(1)}, bf16[2,8,2560]{2,1,0:T(8,128)(2,1)S(1)}, u32[]{:S(2)}, u32[]{:S(2)}) collective-permute-start(bf16[2,8,2560]{2,1,0:T(8,128)(2,1)S(1)} %dynamic-slice_bitcast_fusion.15), channel_id=1, source_target_pairs={{0,8},{4,12},{8,0},{12,4},{16,24},{20,28},{24,16},{28,20},{1,9},{5... | collective-permute-start | bytes 245768 | tf_op jit(solution)/shard_map/ppermute | solution.py:889
  335.2 26.6 %collective-permute-start.32 = (bf16[2,2,2,16,4608]{4,3,0,1,2:T(8,128)(2,1)S(1)}, bf16[2,2,2,16,4608]{4,3,0,1,2:T(8,128)(2,1)}, u32[]{:S(2)}, u32[]{:S(2)}) collective-permute-start(bf16[2,2,2,16,4608]{4,3,0,1,2:T(8,128)(2,1)S(1)} %dynamic-slice_bitcast_fusion), channel_id=1, source_target_pairs={{0,2},{1,3},{2,0},{3,1},{4,6},{5,7},{6,4},{7,5},{8,10},{9,11},{10,... | collective-permute-start | bytes 3538952 | tf_op jit(solution)/shard_map/ppermute | solution.py:889
  338.6 26.0 %collective-permute-start.28 = (bf16[2,2,16,1664]{3,2,0,1:T(8,128)(2,1)S(1)}, bf16[2,2,16,1664]{3,2,0,1:T(8,128)(2,1)S(1)}, u32[]{:S(2)}, u32[]{:S(2)}) collective-permute-start(bf16[2,2,16,1664]{3,2,0,1:T(8,128)(2,1)S(1)} %dynamic-slice_bitcast_fusion.8), channel_id=1, source_target_pairs={{0,4},{4,0},{8,12},{12,8},{16,20},{20,16},{24,28},{28,24},{1,5},{5... | collective-permute-start | bytes 638984 | tf_op jit(solution)/shard_map/ppermute | solution.py:889
  363.7 12.9 %collective-permute-start.33 = (bf16[2,2,16,4608]{3,2,0,1:T(8,128)(2,1)S(1)}, bf16[2,2,16,4608]{3,2,0,1:T(8,128)(2,1)S(1)}, u32[]{:S(2)}, u32[]{:S(2)}) collective-permute-start(bf16[2,2,16,4608]{3,2,0,1:T(8,128)(2,1)S(1)} %dynamic-slice_bitcast_fusion.2), channel_id=1, source_target_pairs={{0,4},{4,0},{8,12},{12,8},{16,20},{20,16},{24,28},{28,24},{1,5},{5... | collective-permute-start | bytes 1769480 | tf_op jit(solution)/shard_map/ppermute | solution.py:889
  364.7 13.9 %collective-permute-start.29 = (bf16[2,16,1664]{2,1,0:T(8,128)(2,1)S(1)}, bf16[2,16,1664]{2,1,0:T(8,128)(2,1)S(1)}, u32[]{:S(2)}, u32[]{:S(2)}) collective-permute-start(bf16[2,16,1664]{2,1,0:T(8,128)(2,1)S(1)} %dynamic-slice_bitcast_fusion.14), channel_id=1, source_target_pairs={{0,8},{4,12},{8,0},{12,4},{16,24},{20,28},{24,16},{28,20},{1,9},{5... | collective-permute-start | bytes 319496 | tf_op jit(solution)/shard_map/ppermute | solution.py:889
  376.8 8.3 %collective-permute-start.34 = (bf16[2,16,4608]{2,1,0:T(8,128)(2,1)S(1)}, bf16[2,16,4608]{2,1,0:T(8,128)(2,1)S(1)}, u32[]{:S(2)}, u32[]{:S(2)}) collective-permute-start(bf16[2,16,4608]{2,1,0:T(8,128)(2,1)S(1)} %dynamic-slice_bitcast_fusion.6), channel_id=1, source_target_pairs={{0,8},{4,12},{8,0},{12,4},{16,24},{20,28},{24,16},{28,20},{1,9},{5... | collective-permute-start | bytes 884744 | tf_op jit(solution)/shard_map/ppermute | solution.py:889
  378.6 9.6 %collective-permute-start.30 = (bf16[16,1664]{1,0:T(8,128)(2,1)S(1)}, bf16[16,1664]{1,0:T(8,128)(2,1)S(1)}, u32[]{:S(2)}, u32[]{:S(2)}) collective-permute-start(bf16[16,1664]{1,0:T(8,128)(2,1)S(1)} %dynamic-slice_bitcast_fusion.17), channel_id=1, source_target_pairs={{0,16},{4,20},{8,24},{12,28},{16,0},{20,4},{24,8},{28,12},{1,17},{... | collective-permute-start | bytes 159752 | tf_op jit(solution)/shard_map/ppermute | solution.py:889
  385.2 7.8 %collective-permute-start.35 = (bf16[16,4608]{1,0:T(8,128)(2,1)S(1)}, bf16[16,4608]{1,0:T(8,128)(2,1)S(1)}, u32[]{:S(2)}, u32[]{:S(2)}) collective-permute-start(bf16[16,4608]{1,0:T(8,128)(2,1)S(1)} %dynamic-slice_bitcast_fusion.10), channel_id=1, source_target_pairs={{0,16},{4,20},{8,24},{12,28},{16,0},{20,4},{24,8},{28,12},{1,17},{... | collective-permute-start | bytes 442376 | tf_op jit(solution)/shard_map/ppermute | solution.py:889
  (41 other events, 532.1 us)
Sparse Core Ops, SparseCore 0:
  17.3 79.1 all-gather.1
